TPU v7x, 512 devices: a whole 4x8x8 slice. The times are simulated.
512 devices in a mesh: dp: 64 (over y, x, core), col: 8 (over z).
Axes of the slice: x: 4, y: 8, z: 8, core: 2. Of those that a mesh axis runs over, the one named last changes fastest.
Arguments:
- gradients: bfloat16 [64, 6, 512, 2048], P('dp', None, None, 'col')
- momentum: float32 [6, 512, 2048], P(None, 'dp', 'col'), may hold values from -48 to 48
- master: float32 [6, 512, 2048], P(None, 'dp', 'col'), may hold values from -0.125 to 0.125
- owners: int32 [6], replicated, may hold values from 0 to 63, as said below
Outputs:
- new_weights: bfloat16 [6, 512, 2048], P(None, None, 'col')
- new_master: float32 [6, 512, 2048], P(None, 'dp', 'col')
- new_momentum: float32 [6, 512, 2048], P(None, 'dp', 'col')
- owned_updates: bfloat16 [64, 2, 512, 2048], P('dp', None, None, 'col')
- owned_rms: float32 [64, 2], P('dp')
Inputs may be any that keep to these rules, and one draw needn't show every extreme that they name: `owners`: no owner index appears more than 2 times, and exactly one appears 2 times.
All inputs are finite; a program needn't handle non-finite values.
Results may differ from a plain program's by a relative error of at most 0.04.
Values may be sent and summed in bfloat16 or wider, within the bound.
A program may use at most 64 MiB of HBM per device.

v0:
```python
import math

import jax
import jax.numpy as jnp
from jax import lax
from jax.sharding import PartitionSpec as P

KV = 512
D = 2048
NS_STEPS = 3
MOST = 2


quintic_first = 3.4445
quintic_second = -4.775
quintic_third = 2.0315
momentum_decay = 0.95
learn_rate = 0.3
weight_decay = 0.1
epsilon = 1e-07


def newton(received):
    iterate = received[0]
    local_sum = jnp.sum(jnp.square(iterate.astype(jnp.float32)), axis=(1, 2))
    squares = lax.psum(local_sum, "col")
    held_rms = jnp.sqrt(squares / float(KV * D))
    iterate = (iterate.astype(jnp.float32) / (jnp.sqrt(squares) + epsilon)[:, None, None]).astype(
        jnp.bfloat16
    )
    for iteration in range(NS_STEPS):
        partial_value = jnp.einsum(
            "sik,sjk->sij", iterate, iterate, preferred_element_type=jnp.float32
        )
        gram_sum = lax.psum(partial_value.astype(jnp.bfloat16), "col").astype(jnp.float32)
        gram_half = gram_sum.astype(jnp.bfloat16)
        square = jnp.einsum(
            "sij,sjk->sik", gram_half, gram_half, preferred_element_type=jnp.float32
        )
        mixing = (quintic_second * gram_sum + quintic_third * square).astype(jnp.bfloat16)
        product = jnp.einsum("sij,sjk->sik", mixing, iterate, preferred_element_type=jnp.float32)
        iterate = (quintic_first * iterate.astype(jnp.float32) + product).astype(jnp.bfloat16)
    factor = 0.2 * math.sqrt(max(KV, D))
    return ((factor * iterate.astype(jnp.float32)).astype(jnp.bfloat16)[None], held_rms[None])


def per_device(gradients, momentum, master, owners):
    dp_count = lax.axis_size("dp")
    terms = gradients[0].astype(jnp.float32)
    summed = lax.psum_scatter(terms, "dp", scatter_dimension=1, tiled=True)
    new_momentum = momentum_decay * momentum + summed
    update = (summed + momentum_decay * new_momentum).astype(jnp.bfloat16)
    matrices = update.shape[0]
    row_count = update.shape[1]
    col_width = update.shape[2]
    matches = owners[:, None] == owners[None, :]
    earlier = (
        jnp.arange(matrices, dtype=jnp.int32)[None, :]
        < jnp.arange(matrices, dtype=jnp.int32)[:, None]
    )
    slot_index = jnp.sum((matches & earlier).astype(jnp.int32), axis=1)
    target = owners * MOST + slot_index
    picker = (jnp.arange(dp_count * MOST, dtype=jnp.int32)[:, None] == target[None, :]).astype(
        jnp.bfloat16
    )
    flat = update.reshape(matrices, row_count * col_width)
    packed = jnp.dot(picker, flat, preferred_element_type=jnp.float32).astype(jnp.bfloat16)
    packed = packed.reshape(dp_count, MOST, row_count, col_width)
    owned_updates, held_rms = newton(
        lax.all_to_all(packed, "dp", split_axis=0, concat_axis=2, tiled=True)
    )
    returned = lax.all_to_all(owned_updates, "dp", split_axis=2, concat_axis=0, tiled=True)
    returned = returned.reshape(dp_count * MOST, row_count * col_width)
    scaled = jnp.dot(picker.T, returned, preferred_element_type=jnp.float32).astype(jnp.bfloat16)
    scaled = scaled.reshape(matrices, row_count, col_width)
    new_master = master * (1.0 - learn_rate * weight_decay) - learn_rate * scaled.astype(
        jnp.float32
    )
    new_weights = lax.all_gather(new_master.astype(jnp.bfloat16), "dp", axis=1, tiled=True)
    return (new_weights, new_master, new_momentum, owned_updates, held_rms)


def solution(mesh):
    return jax.shard_map(
        per_device,
        mesh=mesh,
        in_specs=(P("dp", None, None, "col"), P(None, "dp", "col"), P(None, "dp", "col"), P()),
        out_specs=(
            P(None, None, "col"),
            P(None, "dp", "col"),
            P(None, "dp", "col"),
            P("dp", None, None, "col"),
            P("dp", None),
        ),
        check_vma=False,
    )
```

profile of v0, /device:TPU:1, one launch (start us, length us, event | category | flops | bytes accessed | tf_op | source)
XLA Modules:
  0.0 574.1 jit_solution(13652838069265803181)
XLA Ops:
  7.2 0.0 reduce-scatter.2.cloned.1.call-start
  7.2 3.4 bitcast_convert_fusion
  10.6 0.0 copy-start.3
  10.6 0.0 copy-start.1
  10.6 0.0 reduce-scatter.2.cloned.1.call-update
  10.6 0.0 all-reduce.4.cloned.1.call-start
  10.6 0.6 copy-done.3
  11.2 0.2 convert_reduce_fusion
  11.4 152.1 %reduce-scatter.2.cloned.1.call-done = f32[6,8,256]{2,1,0:T(8,128)} async-done(((f32[6,512,256]{2,1,0:T(8,128)}), f32[6,8,256]{2,1,0:T(8,128)}) %reduce-scatter.2.cloned.1.call-update) | async-done | bytes 49168 | tf_op jit(solution)/shard_map/reduce_scatter | solution.py:50
  163.5 0.0 copy-done.1
  163.5 1.4 fusion.25
  164.9 0.3 convolution_convert_fusion
  165.2 0.1 copy.19
  165.3 30.4 %all_to_all.24 = bf16[64,2,8,256]{3,2,1,0:T(8,128)(2,1)S(1)} all-to-all(bf16[64,2,8,256]{3,2,1,0:T(8,128)(2,1)S(1)} %bitcast.56), channel_id=1, replica_groups=mesh['dp'=64,'col'=8] {'dp'}, dimensions={0} | all-to-all | bytes 1048576 | tf_op jit(solution)/shard_map/all_to_all | solution.py:70
  195.7 0.3 fusion.15
  196.0 14.5 %psum.28 = f32[2]{0:T(128)S(1)} all-reduce(f32[2]{0:T(128)S(1)} %fusion.15), channel_id=1, replica_groups=mesh['dp'=64,'col'=8] {'col'}, use_global_device_ids=true, to_apply=%region_3.0 | all-reduce | flops 2 | bytes 16 | tf_op jit(solution)/shard_map/psum | solution.py:26
  210.5 0.5 sqrt_bitcast_fusion
  211.0 1.5 convolution_convert_fusion.4
  212.5 0.0 all-reduce.4.cloned.1.call-update
  212.5 0.0 all-reduce.6.cloned.1.call-start
  212.6 75.5 %all-reduce.4.cloned.1.call-done = bf16[2,512,512]{2,1,0:T(8,128)(2,1)} async-done(((bf16[2,512,512]{2,1,0:T(8,128)(2,1)}), bf16[2,512,512]{2,1,0:T(8,128)(2,1)}) %all-reduce.4.cloned.1.call-update) | async-done | bytes 1048592 | tf_op jit(solution)/shard_map/psum | solution.py:35
  288.1 3.1 fusion.8
  291.2 1.4 convolution_convert_fusion.3
  292.6 0.0 all-reduce.6.cloned.1.call-update
  292.6 0.0 all-reduce.8.cloned.1.call-start
  292.7 80.3 %all-reduce.6.cloned.1.call-done = bf16[2,512,512]{2,1,0:T(8,128)(2,1)} async-done(((bf16[2,512,512]{2,1,0:T(8,128)(2,1)}), bf16[2,512,512]{2,1,0:T(8,128)(2,1)}) %all-reduce.6.cloned.1.call-update) | async-done | bytes 1048592 | tf_op jit(solution)/shard_map/psum | solution.py:35
  373.0 3.0 fusion.9
  376.0 1.4 convolution_convert_fusion.2
  377.5 0.0 all-reduce.8.cloned.1.call-update
  377.5 0.0 all-gather.2.cloned.1.call-start
  377.6 80.3 %all-reduce.8.cloned.1.call-done = bf16[2,512,512]{2,1,0:T(8,128)(2,1)} async-done(((bf16[2,512,512]{2,1,0:T(8,128)(2,1)}), bf16[2,512,512]{2,1,0:T(8,128)(2,1)}) %all-reduce.8.cloned.1.call-update) | async-done | bytes 1048592 | tf_op jit(solution)/shard_map/psum | solution.py:35
  457.8 3.0 fusion.14
  460.9 0.0 copy-start
  460.9 0.5 copy.16
  461.4 0.0 copy-start.2
  461.4 31.8 %all_to_all.25 = bf16[1,2,512,256]{3,1,0,2:T(2,128)(2,1)S(1)} all-to-all(bf16[1,2,512,256]{3,1,0,2:T(2,128)(2,1)S(1)} %copy.16), channel_id=1, replica_groups=mesh['dp'=64,'col'=8] {'dp'}, dimensions={2} | all-to-all | bytes 1048576 | tf_op jit(solution)/shard_map/all_to_all | solution.py:72
  493.3 0.1 copy.17
  493.4 0.1 copy.20
  493.5 0.0 copy-done
  493.5 0.2 fusion.1
  493.7 0.0 copy-done.2
  493.7 0.7 fusion.35
  494.4 0.0 all-gather.2.cloned.1.call-update
  494.4 70.6 %all-gather.2.cloned.1.call-done = bf16[6,512,256]{2,1,0:T(8,128)(2,1)} async-done(((bf16[6,8,256]{2,1,0:T(8,128)(2,1)}), bf16[6,512,256]{2,1,0:T(8,128)(2,1)}) %all-gather.2.cloned.1.call-update) | async-done | bytes 1572880 | tf_op jit(solution)/shard_map/all_gather | solution.py:79
  565.0 2.7 copy.34
  (2 shorter events, 0.0 us)
Async XLA Ops:
  7.2 156.3 %reduce-scatter.2.cloned.1.call-start = ((), (), s32[]{:S(2)}) async-start(), calls=%async_computation.3 | async-start | bytes 3194880 | tf_op jit(solution)/shard_map/reduce_scatter | solution.py:50
  10.6 0.7 copy-start.3
  10.6 152.9 %copy-start.1 = (f32[6,8,256]{2,1,0:T(8,128)S(1)}, f32[6,8,256]{2,1,0:T(8,128)}, u32[]{:S(2)}) copy-start(f32[6,8,256]{2,1,0:T(8,128)} %param.5) | copy-start | bytes 147460
  10.6 277.5 %all-reduce.4.cloned.1.call-start = ((), (), s32[]{:S(2)}) async-start(), calls=%async_computation.4 | async-start | bytes 2097152 | tf_op jit(solution)/shard_map/psum | solution.py:35
  212.5 160.5 %all-reduce.6.cloned.1.call-start = ((), (), s32[]{:S(2)}) async-start(), calls=%async_computation.5 | async-start | bytes 2097152 | tf_op jit(solution)/shard_map/psum | solution.py:35
  292.6 165.2 %all-reduce.8.cloned.1.call-start = ((), (), s32[]{:S(2)}) async-start(), calls=%async_computation.6 | async-start | bytes 2097152 | tf_op jit(solution)/shard_map/psum | solution.py:35
  377.5 187.5 %all-gather.2.cloned.1.call-start = ((), (), s32[]{:S(2)}) async-start(), calls=%async_computation.7 | async-start | bytes 1597440 | tf_op jit(solution)/shard_map/all_gather | solution.py:79
  460.9 32.6 %copy-start = (bf16[1,2,512,256]{3,2,1,0:T(8,128)(2,1)}, bf16[1,2,512,256]{3,2,1,0:T(8,128)(2,1)S(1)}, u32[]{:S(2)}) copy-start(bf16[1,2,512,256]{3,2,1,0:T(8,128)(2,1)S(1)} %fusion.14) | copy-start | bytes 1572868
  461.4 32.3 %copy-start.2 = (f32[6,8,256]{2,1,0:T(8,128)S(1)}, f32[6,8,256]{2,1,0:T(8,128)}, u32[]{:S(2)}) copy-start(f32[6,8,256]{2,1,0:T(8,128)} %param.6) | copy-start | bytes 147460
Sparse Core Ops, SparseCore 0:
  12.7 150.7 reduce-scatter.1
  212.7 75.3 all-reduce.3
  292.8 80.1 all-reduce.5
  377.6 80.1 all-reduce.7
  494.5 70.3 all-gather.1
where the time goes:
time: 575 us; the launch traced here: 574 us
  waiting for transfers between devices  459 us (80%)
  blocking collectives  76.7 us (13%)
  matrix products  14.1 us (2%)
  between operations  13.9 us (2%)
  other arithmetic  6.4 us (1%)
    psum x3, waiting for transfers between devices, newton(): lax.psum(partial_value.astype(jnp.bfloat16), 'col').astype(jnp.float32)  236 us
    reduce_scatter x1, waiting for transfers between devices, per_device(): summed = lax.psum_scatter(terms, 'dp', scatter_dimension=1, tiled=True)  152 us
    all_gather x1, waiting for transfers between devices, per_device(): lax.all_gather(new_master.astype(jnp.bfloat16), 'dp', axis=1, tiled=True)  70.6 us
    all_to_all x1, blocking collectives, per_device(): lax.all_to_all(owned_updates, 'dp', split_axis=2, concat_axis=0, tiled=True)  31.8 us
    all_to_all x1, blocking collectives, per_device(): lax.all_to_all(packed, 'dp', split_axis=0, concat_axis=2, tiled=True)  30.4 us
    psum x1, blocking collectives, newton(): squares = lax.psum(local_sum, 'col')  14.5 us
  transfers between devices with their start and end apart: 5, of which 5 were waited for; matrix products, arithmetic and copies ran while one was open for 0% of the time, Pallas kernels for 0%

commit v1 on v0

v1 whole, which is shorter than its diff:
```python
import functools
import math

import jax
import jax.numpy as jnp
from jax import lax
from jax.experimental import pallas as pl
from jax.experimental.pallas import tpu as pltpu
from jax.sharding import PartitionSpec as P

KV = 512
D = 2048
NM = 6
MOST = 2
NY = 8
NX = 4
NZ = 8

quintic_first = 3.4445
quintic_second = -4.775
quintic_third = 2.0315
momentum_decay = 0.95
learn_rate = 0.3
weight_decay = 0.1
epsilon = 1e-07
factor = 0.2 * math.sqrt(max(KV, D))

f32 = jnp.float32
bf16 = jnp.bfloat16
HALF = 3

BUFFERS = dict(
    own_g=((NM, KV, 128), bf16),
    sib_g=((NM, KV, 128), bf16),
    sum1=((NX, NM, 128, 128), bf16),
    xr=((NX - 1, NM, 128, 128), bf16),
    sum2=((NM, 128, 128), bf16),
    yr=((NY - 1, 128, 128), bf16),
    mom16=((NM, 16, 128), f32),
    mas16=((NM, 16, 128), f32),
    masb=((NM, 16, 128), bf16),
    momr=((NY, 16, 128), f32),
    nmw=((NY, 16, 128), f32),
    nm16=((NM, 16, 128), f32),
    nmsib=((NM, 8, 128), f32),
    u=((NX, 128, 128), bf16),
    gps=((64, 512), bf16),
    gpk=((64, 512), f32),
    gpr=((64, 512), bf16),
    gzs=((NZ, 16, 256), bf16),
    gzr=((NZ - 1, 16, 256), bf16),
    gz=((NZ, 16, 256), bf16),
    g4=((2, NX, 64, 512), bf16),
    gb=((512, 512), bf16),
    m0=((512, 512), bf16),
    m1=((512, 512), bf16),
    g2f=((512, 512), f32),
    g2b=((512, 512), bf16),
    sqw=((8, 128), f32),
    big=((2, NX, NM, 128, 128), bf16),
    mb=((2, NX, NY, NM, 16, 128), bf16),
)
PHASES = dict(
    loc=3, sg=1, smo=1, sma=1, x1=3, y1=7, my=7, ay=7, ux=3, gs=1, zr=7, za=7, gx=3, gc=1,
    ax=3, ac=4, ny=8, ns=1, sq=8, sy=8, sx=6, sc=8,
)


def kernel(g, mom, mas, w_out, s_out, nm_out, sq_out, *scratch):
    names = list(BUFFERS)
    B = dict(zip(names, scratch[: len(names)]))
    sems = scratch[len(names):]
    S = {p: (sems[2 * i], sems[2 * i + 1]) for i, p in enumerate(PHASES)}

    d = lax.axis_index("dp")
    z = lax.axis_index("col")
    c = d % 2
    x = (d // 2) % NX
    y = d // 8
    oc = 1 - c
    worker = y < NM

    def dev(yy, xx, cc, zz):
        return ((yy * NX + xx) * 2 + cc, zz)

    sib = dev(y, x, oc, z)

    def xpeer(k):
        return dev(y, (x + k) % NX, c, z)

    def ypeer(k):
        return dev((y + k) % NY, x, c, z)

    def zpeer(k):
        return dev(y, x, c, (z + k) % NZ)

    def remote(phase, i, src, dst, to, send=None):
        return pltpu.make_async_remote_copy(
            src_ref=src,
            dst_ref=dst,
            send_sem=S[phase][0].at[i if send is None else send],
            recv_sem=S[phase][1].at[i],
            device_id=to,
            device_id_type=pl.DeviceIdType.MESH,
        )

    def local(i, src, dst):
        return pltpu.make_async_copy(src, dst, S["loc"][0].at[i])

    def cols(cc):
        return pl.ds(pl.multiple_of(cc * 128, 128), 128)

    def rows8(cc):
        return pl.ds(pl.multiple_of(cc * 8, 8), 8)

    loc = [
        local(0, g.at[:, :, cols(c)], B["own_g"]),
        local(1, mom.at[:, :, cols(c)], B["mom16"].at[:, rows8(c), :]),
        local(2, mas.at[:, :, cols(c)], B["mas16"].at[:, rows8(c), :]),
    ]
    for item in loc:
        item.start()

    barrier = pltpu.get_barrier_semaphore()
    partners = [sib] + [xpeer(k) for k in range(1, NX)]
    partners += [ypeer(k) for k in range(1, NY)] + [zpeer(k) for k in range(1, NZ)]
    for to in partners:
        pl.semaphore_signal(barrier, inc=1, device_id=to, device_id_type=pl.DeviceIdType.MESH)
    pl.semaphore_wait(barrier, len(partners))

    sg = remote("sg", 0, g.at[:, :, cols(oc)], B["sib_g"], sib)
    smo = remote("smo", 0, mom.at[:, :, cols(oc)], B["mom16"].at[:, rows8(c), :], sib)
    sma = remote("sma", 0, mas.at[:, :, cols(oc)], B["mas16"].at[:, rows8(c), :], sib)
    sg.start()
    smo.start()
    sma.start()
    for item in loc:
        item.wait()
    sg.wait_recv()

    def add_pair(k):
        xx = (x + k) % NX

        def one(m, carry):
            for yy in range(NY):
                rows = pl.ds(pl.multiple_of(yy * 64 + xx * 16, 16), 16)
                total = B["own_g"][m, rows, :].astype(f32) + B["sib_g"][m, rows, :].astype(f32)
                B["sum1"][xx, m, pl.ds(yy * 16, 16), :] = total.astype(bf16)
            return carry

        lax.fori_loop(0, NM, one, 0)

    def x1(k):
        return remote("x1", k - 1, B["sum1"].at[(x + k) % NX], B["xr"].at[k - 1], xpeer(k))

    for k in (2, 1, 3):
        add_pair(k)
        x1(k).start()
    add_pair(0)

    smo.wait_recv()
    sma.wait_recv()

    def my(m):
        slot = (m - y + NY) % NY - 1
        return remote("my", slot, B["mom16"].at[m], B["momr"].at[y], dev(m, x, c, z))

    for m in range(NM):
        @pl.when(y != m)
        def _(m=m):
            my(m).start()

        @pl.when(y == m)
        def _(m=m):
            B["momr"][m] = B["mom16"][m]

    B["masb"][...] = B["mas16"][...].astype(bf16)

    for k in range(1, NX):
        x1(k).wait_recv()

    def y1(m):
        slot = (m - y + NY) % NY - 1
        return remote("y1", slot, B["sum2"].at[m], B["yr"].at[slot], dev(m, x, c, z))

    for m in range(NM):
        total = B["sum1"][x, m].astype(f32)
        for k in range(1, NX):
            total = total + B["xr"][k - 1, m].astype(f32)
        B["sum2"][m] = total.astype(bf16)

        @pl.when(y != m)
        def _(m=m):
            y1(m).start()

    def ay(k):
        return remote("ay", k - 1, B["masb"], B["mb"].at[c, x, y], ypeer(k))

    for k in range(1, NY):
        ay(k).start()
    B["mb"][c, x, y] = B["masb"][...]

    def ux(k):
        return remote("ux", k - 1, B["u"].at[x], B["u"].at[x], xpeer(k))

    def ny(yy):
        return remote("ny", y, B["nmw"].at[yy], B["nm16"].at[y], dev(yy, x, c, z), send=yy)

    gs = remote("gs", 0, B["gps"], B["gpr"], sib)

    def zr(k):
        return remote("zr", k - 1, B["gzs"].at[(z + k) % NZ], B["gzr"].at[k - 1], zpeer(k))

    def za(k):
        return remote("za", k - 1, B["gz"].at[z], B["gz"].at[z], zpeer(k))

    def gx(k):
        return remote("gx", k - 1, B["g4"].at[c, x], B["g4"].at[c, x], xpeer(k))

    gc = remote("gc", 0, B["g4"].at[c], B["g4"].at[c], sib)

    def dot(left, right):
        return jnp.dot(left, right, preferred_element_type=f32)

    @pl.when(worker)
    def _():
        for k in range(1, NY):
            pltpu.make_async_remote_copy(
                src_ref=B["mom16"].at[0], dst_ref=B["momr"].at[0],
                send_sem=S["my"][0].at[k - 1], recv_sem=S["my"][1].at[k - 1],
                device_id=sib, device_id_type=pl.DeviceIdType.MESH,
            ).wait_recv()
        for k in range(1, NY):
            pltpu.make_async_remote_copy(
                src_ref=B["sum2"].at[0], dst_ref=B["yr"].at[k - 1],
                send_sem=S["y1"][0].at[k - 1], recv_sem=S["y1"][1].at[k - 1],
                device_id=sib, device_id_type=pl.DeviceIdType.MESH,
            ).wait_recv()
        summed = B["sum2"][y].astype(f32)
        for k in range(1, NY):
            summed = summed + B["yr"][k - 1].astype(f32)
        new_mom = momentum_decay * B["momr"][...].reshape(128, 128) + summed
        B["u"][x] = (summed + momentum_decay * new_mom).astype(bf16)
        for k in (2, 1, 3):
            ux(k).start()
        B["nmw"][...] = new_mom.reshape(NY, 16, 128)
        for yy in range(NY):
            @pl.when(y != yy)
            def _(yy=yy):
                ny(yy).start()

        B["nm16"][y] = B["nmw"][y]
        for k in range(1, NX):
            ux(k).wait_recv()

        full = B["u"][...].reshape(KV, 128)
        part = lax.dot_general(
            B["u"][x], full, (((1,), (1,)), ((), ())), preferred_element_type=f32
        )
        mine = pl.ds(pl.multiple_of(c * 64, 64), 64)
        B["g2f"][0:128, :] = part
        B["gps"][...] = B["g2f"][pl.ds(pl.multiple_of(oc * 64, 64), 64), :].astype(bf16)
        gs.start()
        gs.wait_recv()
        B["gpk"][...] = B["g2f"][mine, :] + B["gpr"][...].astype(f32)
        for p in range(NZ):
            B["gzs"][p] = B["gpk"][
                (p // 2) * 16:(p // 2) * 16 + 16, (p % 2) * 256:(p % 2) * 256 + 256
            ].astype(bf16)
        for k in (4, 3, 5, 2, 6, 1, 7):
            zr(k).start()

    for k in range(1, NY):
        ay(k).wait_recv()

    def ax(k):
        return remote("ax", k - 1, B["mb"].at[c, x], B["mb"].at[c, x], xpeer(k))

    for k in range(1, NX):
        ax(k).start()

    @pl.when(worker)
    def _():
        for k in range(1, NZ):
            zr(k).wait_recv()
        total = B["gzs"][z].astype(f32)
        for k in range(1, NZ):
            total = total + B["gzr"][k - 1].astype(f32)
        B["gz"][z] = total.astype(bf16)
        for k in (4, 3, 5, 2, 6, 1, 7):
            za(k).start()
        for k in range(1, NZ):
            za(k).wait_recv()
        for p in range(NZ):
            B["g4"][
                c, x, (p // 2) * 16:(p // 2) * 16 + 16, (p % 2) * 256:(p % 2) * 256 + 256
            ] = B["gz"][p]
        for k in (2, 1, 3):
            gx(k).start()
        for k in range(1, NX):
            gx(k).wait_recv()
        gc.start()
        gc.wait_recv()

    for k in range(1, NX):
        ax(k).wait_recv()

    def ac(k):
        xx = (x + k) % NX
        return remote("ac", k, B["mb"].at[c, xx], B["mb"].at[c, xx], sib)

    for k in range(NX):
        ac(k).start()

    def sy(yy):
        return remote("sy", y, B["big"].at[c, x, y], B["big"].at[c, x, y], dev(yy, x, c, z), send=yy)

    def sq(yy):
        return remote("sq", y, B["sqw"], sq_out.at[y], dev(yy, x, c, z), send=yy)

    @pl.when(worker)
    def _():
        for xx in range(NX):
            for cc in range(2):
                at = (xx * 2 + cc) * 64
                B["g2f"][at:at + 64, :] = B["g4"][cc, xx].astype(f32)
        gram = B["g2f"][...]
        diagonal = lax.broadcasted_iota(jnp.int32, (512, 512), 0) == lax.broadcasted_iota(
            jnp.int32, (512, 512), 1
        )
        squares = jnp.sum(
            jnp.sum(jnp.where(diagonal, gram, 0.0), axis=0, keepdims=True), axis=1, keepdims=True
        )
        B["sqw"][...] = jnp.broadcast_to(squares, (8, 128))
        for yy in range(NY):
            @pl.when(y != yy)
            def _(yy=yy):
                sq(yy).start()
        sq_out[y] = B["sqw"][...]
        scale = 1.0 / (jnp.sqrt(squares) + epsilon)

        gram = (gram * scale) * scale

        def mixing(gram, half):
            return (quintic_second * gram + quintic_third * dot(half, half)).astype(bf16)

        def advance(gram, half, mix):
            once = quintic_first * gram + dot(mix, half)
            return quintic_first * once + dot(once.astype(bf16), mix)

        B["gb"][...] = gram.astype(bf16)
        B["m0"][...] = mixing(gram, B["gb"][...])
        gram = advance(gram, B["gb"][...], B["m0"][...])
        B["gb"][...] = gram.astype(bf16)
        B["m1"][...] = mixing(gram, B["gb"][...])
        gram = advance(gram, B["gb"][...], B["m1"][...])
        B["g2f"][...] = gram
        B["g2b"][...] = gram.astype(bf16)
        mine = pl.ds(pl.multiple_of(x * 128, 128), 128)
        mix2 = (
            quintic_second * B["g2f"][mine, :]
            + quintic_third * dot(B["g2b"][mine, :], B["g2b"][...])
        ).astype(bf16)
        k1 = quintic_first * (B["m1"][mine, :].astype(f32) + mix2.astype(f32)) + dot(
            mix2, B["m1"][...]
        )
        k0 = (
            quintic_first**2 * B["m0"][mine, :].astype(f32)
            + quintic_first * k1
            + dot(k1.astype(bf16), B["m0"][...])
        )
        last = quintic_first**3 * B["u"][x].astype(f32) + dot(
            k0.astype(bf16), B["u"][...].reshape(KV, 128)
        )
        last = (last * scale).astype(bf16)
        B["big"][c, x, y] = (factor * last.astype(f32)).astype(bf16)
        for k in (4, 3, 5, 2, 6, 1, 7):
            sy((y + k) % NY).start()

    for m in range(NM):
        @pl.when(y != m)
        def _(m=m):
            remote("ny", m, B["nmw"].at[0], B["nm16"].at[m], sib).wait_recv()

    ns = remote("ns", 0, B["nm16"].at[:, rows8(oc), :], B["nmsib"], sib)
    ns.start()
    nm_out[:, :, cols(c)] = B["nm16"][:, rows8(c), :]

    def sx(h, k):
        part = B["big"].at[c, x, pl.ds(h * HALF, HALF)]
        return remote("sx", h * 3 + k - 1, part, part, xpeer(k))

    def sc(h, k):
        part = B["big"].at[c, (x + NX - k) % NX, pl.ds(h * HALF, HALF)]
        return remote("sc", h * 4 + k, part, part, sib)

    for h in range(2):
        for m in range(h * HALF, h * HALF + HALF):
            @pl.when(y != m)
            def _(m=m):
                remote("sy", m, B["big"].at[c, x, m], B["big"].at[c, x, m], sib).wait_recv()
        for k in (2, 1, 3):
            sx(h, k).start()
        sc(h, 0).start()
    ns.wait_recv()
    nm_out[:, :, cols(oc)] = B["nmsib"][...]
    for k in range(NX):
        ac(k).wait_recv()
    for m in range(NM):
        @pl.when(y != m)
        def _(m=m):
            remote("sq", m, B["sqw"], sq_out.at[m], sib).wait_recv()

    def finish(cc, xx, h):
        def one(m, carry):
            for yy in range(NY):
                rows = pl.ds(pl.multiple_of(yy * 64 + xx * 16, 16), 16)
                scaled = B["big"][cc, xx, m, pl.ds(yy * 16, 16), :]
                master = B["mb"][cc, xx, yy, m].astype(f32)
                s_out[m, rows, cols(cc)] = scaled
                w_out[m, rows, cols(cc)] = (
                    master * (1.0 - learn_rate * weight_decay) - learn_rate * scaled.astype(f32)
                ).astype(bf16)
            return carry

        lax.fori_loop(h * HALF, h * HALF + HALF, one, 0)

    for h in range(2):
        for k in (1, 3, 2):
            sx(h, k).wait_recv()
            sc(h, k).start()
    for h in range(2):
        for k in range(NX):
            finish(c, (x + k) % NX, h)
    for h in range(2):
        for k in range(NX):
            sc(h, k).wait_recv()
            finish(oc, (x + NX - k) % NX, h)

    sg.wait_send()
    smo.wait_send()
    sma.wait_send()
    for k in range(1, NX):
        x1(k).wait_send()
        ax(k).wait_send()
    for k in range(1, NY):
        ay(k).wait_send()
    for k in range(NX):
        ac(k).wait_send()
    ns.wait_send()
    for h in range(2):
        for k in range(1, NX):
            sx(h, k).wait_send()
        for k in range(NX):
            sc(h, k).wait_send()
    for m in range(NM):
        @pl.when(y != m)
        def _(m=m):
            my(m).wait_send()
            y1(m).wait_send()

    @pl.when(worker)
    def _():
        for k in range(1, NX):
            ux(k).wait_send()
            gx(k).wait_send()
        gs.wait_send()
        gc.wait_send()
        for k in range(1, NZ):
            zr(k).wait_send()
            za(k).wait_send()
        for yy in range(NY):
            @pl.when(y != yy)
            def _(yy=yy):
                ny(yy).wait_send()
                sq(yy).wait_send()
                sy(yy).wait_send()


def step(g, mom, mas):
    vmem = pl.BlockSpec(memory_space=pltpu.VMEM)
    scratch = [pltpu.VMEM(*spec) for spec in BUFFERS.values()]
    for count in PHASES.values():
        scratch += [pltpu.SemaphoreType.DMA((count,)), pltpu.SemaphoreType.DMA((count,))]
    return pl.pallas_call(
        kernel,
        out_shape=(
            jax.ShapeDtypeStruct((NM, KV, 256), bf16),
            jax.ShapeDtypeStruct((NM, KV, 256), bf16),
            jax.ShapeDtypeStruct((NM, 8, 256), f32),
            jax.ShapeDtypeStruct((NM, 8, 128), f32),
        ),
        in_specs=[pl.BlockSpec(memory_space=pl.ANY), vmem, vmem],
        out_specs=(vmem, vmem, vmem, vmem),
        scratch_shapes=scratch,
        compiler_params=pltpu.CompilerParams(
            collective_id=0, has_side_effects=True, vmem_limit_bytes=48 * 1024 * 1024
        ),
        name="muon_step",
    )(g, mom, mas)


def per_device(gradients, momentum, master, owners):
    new_weights, scaled, new_momentum, squares = step(gradients[0], momentum, master)
    me = lax.axis_index("dp")
    matches = owners[:, None] == owners[None, :]
    order = jnp.arange(NM, dtype=jnp.int32)
    slot = jnp.sum((matches & (order[None, :] < order[:, None])).astype(jnp.int32), axis=1)
    picker = (owners[None, :] == me) & (
        slot[None, :] == jnp.arange(MOST, dtype=jnp.int32)[:, None]
    )
    held = jnp.any(picker, axis=1)
    which = jnp.argmax(picker, axis=1)
    owned = [
        jnp.where(
            held[s], lax.dynamic_index_in_dim(scaled, which[s], 0, keepdims=False), jnp.zeros((), bf16)
        )
        for s in range(MOST)
    ]
    owned_updates = jnp.stack(owned)[None]
    rms = jnp.sqrt(squares[:, 0, 0] / float(KV * D))
    held_rms = jnp.sum(jnp.where(picker, rms[None, :], 0.0), axis=1)[None]
    rows = lax.dynamic_slice_in_dim(scaled, me * 8, 8, axis=1)
    new_master = master * (1.0 - learn_rate * weight_decay) - learn_rate * rows.astype(f32)
    return (new_weights, new_master, new_momentum, owned_updates, held_rms)


def solution(mesh):
    return jax.shard_map(
        per_device,
        mesh=mesh,
        in_specs=(P("dp", None, None, "col"), P(None, "dp", "col"), P(None, "dp", "col"), P()),
        out_specs=(
            P(None, None, "col"),
            P(None, "dp", "col"),
            P(None, "dp", "col"),
            P("dp", None, None, "col"),
            P("dp", None),
        ),
        check_vma=False,
    )
```

time: 575 us -> 99.6 us (0.17)
  waiting for transfers between devices: 459 us -> 0 us
  Pallas kernels: 0 us -> 82.9 us
  blocking collectives: 76.7 us -> 0 us
  matrix products: 14.1 us -> 0 us
  between operations: 13.9 us -> 4.54 us
    psum x3 -> x0, waiting for transfers between devices: 236 us -> none  [newton(): lax.psum(partial_value.astype(jnp.bfloat16), 'col').astype(jnp.float32)]
    reduce_scatter x1 -> x0, waiting for transfers between devices: 152 us -> none  [per_device(): summed = lax.psum_scatter(terms, 'dp', scatter_dimension=1, tiled=True)]
    pallas_call x0 -> x1, Pallas kernels: none -> 82.9 us  [step(): pl.pallas_call(kernel, out_shape=(jax.ShapeDtypeStruct((NM, KV, 256), bf1...]
    all_gather x1 -> x0, waiting for transfers between devices: 70.6 us -> none  [per_device(): lax.all_gather(new_master.astype(jnp.bfloat16), 'dp', axis=1, tiled=True)]
    all_to_all x2 -> x0, blocking collectives: 62.2 us -> none  [the longest x1 31.8 us: per_device(): lax.all_to_all(owned_updates, 'dp', split_axis=2, concat_axis=0, tiled=True)]
    psum x1 -> x0, blocking collectives: 14.5 us -> none  [newton(): squares = lax.psum(local_sum, 'col')]
    dot_general x8 -> x0, matrix products: 14.1 us -> none  [the longest x3 9.15 us: newton(): jnp.einsum('sij,sjk->sik', mixing, iterate, preferred_element_type=jnp.fl...]
  transfers between devices with their start and end apart: 5 -> 0, of which waited for: 5 -> 0; matrix products, arithmetic and copies ran while one was open for 0% -> 0% of each run, Pallas kernels for 0% -> 0%
where the time goes in v1:
time: 99.6 us; the launch traced here: 99.3 us
  Pallas kernels  82.9 us (83%)
  local copies, waits for them, and re-layouts  5.94 us (6%)
  other arithmetic  5.9 us (6%)
  between operations  4.54 us (5%)
    pallas_call x1, Pallas kernels, step(): pl.pallas_call(kernel, out_shape=(jax.ShapeDtypeStruct((NM, KV, 256), bf1...  82.9 us
    unnamed x10, local copies, waits for them, and re-layouts  4.77 us

profile of v1, /device:TPU:1, one launch (start us, length us, event | category | flops | bytes accessed | tf_op | source)
XLA Modules:
  0.0 99.3 jit_solution(8111088494543843062)
XLA Ops:
  0.6 0.7 broadcast_compare_fusion
  1.3 0.9 convert_reduce_fusion
  2.2 0.6 iota_reduce_fusion
  2.8 0.6 fusion.3
  7.3 0.1 fusion.1
  7.4 0.6 fusion.2
  8.0 0.0 copy-start
  8.0 1.4 %copy-done = bf16[1,6,512,256]{3,2,1,0:T(8,128)(2,1)S(1)} copy-done((bf16[1,6,512,256]{3,2,1,0:T(8,128)(2,1)S(1)}, bf16[1,6,512,256]{3,2,1,0:T(8,128)(2,1)}, u32[]{:S(2)}) %copy-start) | copy-done | bytes 1572888
  9.4 0.0 copy-start.1
  9.4 0.8 copy-done.1
  10.2 0.0 copy-start.3
  10.2 0.8 copy-done.3
  11.0 0.0 copy-start.2
  11.0 82.9 %muon_step.1 = (bf16[6,512,256]{2,1,0:T(8,128)(2,1)S(1)}, bf16[6,512,256]{2,1,0:T(8,128)(2,1)S(1)}, f32[6,8,256]{2,1,0:T(8,128)S(1)}, f32[6,8,128]{2,1,0:T(8,128)S(1)}) custom-call(bf16[6,512,256]{2,1,0:T(8,128)(2,1)S(1)} %bitcast.8, f32[6,8,256]{2,1,0:T(8,128)S(1)} %copy-done.3, f32[6,8,256]{2,1,0:T(8,128)S(1)} %copy-done.1), custom_call_target="tpu_custom_call" | custom-call | tf_op jit(solution)/shard_map/muon_step/pallas_call | solution.py:485
  93.9 1.3 %dynamic-slice_select_fusion.1 = (bf16[1,512,256]{2,1,0:T(8,128)(2,1)S(1)}, bf16[1,512,256]{2,1,0:T(8,128)(2,1)S(1)}) fusion(bf16[6,512,256]{2,1,0:T(8,128)(2,1)S(1)} %get-tuple-element.11, s32[]{:T(128)S(6)} %select_n.36, pred[]{:T(512)} %bitcast.1, s32[]{:T(128)S(6)} %select_n.39, pred[]{:T(512)} %bitcast.3), kind=kLoop, calls=%fused_computation.2 | loop fusion | flops 262144 | bytes 1048586 | tf_op jit(solution)/shard_map/jit(_where)/select_n | solution.py:515
  95.2 0.8 maximum_bitcast_fusion
  96.1 0.0 copy-done.2
  96.1 0.6 multiply_subtract_fusion
  96.7 0.1 sqrt_reduce_fusion
  96.9 0.6 select_reduce_fusion
  97.5 1.1 %copy.11 = bf16[6,512,256]{2,1,0:T(8,128)(2,1)} copy(bf16[6,512,256]{2,1,0:T(8,128)(2,1)S(1)} %get-tuple-element.26) | data formatting | bytes 3145728
  98.6 0.6 copy.12
Async XLA Ops:
  8.0 1.4 %copy-start = (bf16[1,6,512,256]{3,2,1,0:T(8,128)(2,1)S(1)}, bf16[1,6,512,256]{3,2,1,0:T(8,128)(2,1)}, u32[]{:S(2)}) copy-start(bf16[1,6,512,256]{3,2,1,0:T(8,128)(2,1)} %param.4) | copy-start | bytes 4718596
  9.4 0.8 copy-start.1
  10.2 0.8 copy-start.3
  11.0 85.1 %copy-start.2 = (f32[6,8,256]{2,1,0:T(8,128)S(1)}, f32[6,8,256]{2,1,0:T(8,128)}, u32[]{:S(2)}) copy-start(f32[6,8,256]{2,1,0:T(8,128)} %mas.1) | copy-start | bytes 147460

commit v2 on v0

v2 whole, which is shorter than its diff:
```python
import functools
import math

import jax
import jax.numpy as jnp
from jax import lax
from jax.experimental import pallas as pl
from jax.experimental.pallas import tpu as pltpu
from jax.sharding import PartitionSpec as P

KV = 512
D = 2048
NM = 6
MOST = 2
NY = 8
NX = 4
NZ = 8

quintic_first = 3.4445
quintic_second = -4.775
quintic_third = 2.0315
momentum_decay = 0.95
learn_rate = 0.3
weight_decay = 0.1
epsilon = 1e-07
factor = 0.2 * math.sqrt(max(KV, D))

f32 = jnp.float32
bf16 = jnp.bfloat16
ORDER = (0, 3, 1, 4, 2, 5)

BUFFERS = dict(
    own_g=((NM, KV, 128), bf16),
    sib_g=((NM, KV, 128), bf16),
    sum1=((NM, NX, 128, 128), bf16),
    xr=((NM, NX - 1, 128, 128), bf16),
    sum2=((NM, 128, 128), bf16),
    yr=((NY - 1, 128, 128), bf16),
    mas=((NM, 8, 256), f32),
    mom16=((NM, 16, 128), f32),
    mas16=((NM, 16, 128), f32),
    masb=((NM, 16, 128), bf16),
    momr=((NY, 16, 128), f32),
    nmw=((NY, 16, 128), f32),
    nm16=((NM, 16, 128), f32),
    nmsib=((NM, 8, 128), f32),
    u=((NX, 128, 128), bf16),
    part=((128, 512), f32),
    gps=((64, 512), bf16),
    gpr=((64, 512), bf16),
    gzs=((NZ, 16, 256), bf16),
    gzr=((NZ - 1, 16, 256), bf16),
    gz=((NZ, 16, 256), bf16),
    g4=((2, NX, 64, 512), bf16),
    gf=((512, 512), f32),
    gb=((512, 512), bf16),
    m0=((512, 512), bf16),
    m1=((512, 512), bf16),
    sqw=((8, 128), f32),
    sqr=((NM, 8, 128), f32),
    big=((2, NM, NX, 128, 128), bf16),
    mb=((2, NX, NY, NM, 16, 128), bf16),
    w=((NM, KV, 256), bf16),
    ow=((MOST, KV, 256), bf16),
)
PHASES = dict(
    loc=(4, 1), out=(1, 1), sg=(NM, NM), smo=(1, 1), sma=(1, 1), x1=(1, NM), y1=(7, 1), my=(7, 1),
    ay=(1, 1), ux=(1, 1), gs=(1, 1), zr=(1, 1), za=(1, 1), gx=(1, 1), gc=(1, 1), ax=(1, 1),
    ac=(1, 1), ny=(8, NM), ns=(1, 1), sq=(8, NM), sy=(1, NM), sx=(1, NM), sc=(1, NM),
)


def stages(owners, g, mom, mas, w_out, nm_out, ma_out, ow_out, rms_out, *scratch):
    names = list(BUFFERS)
    B = dict(zip(names, scratch[: len(names)]))
    sems = scratch[len(names):]
    S = {p: (sems[2 * i], sems[2 * i + 1]) for i, p in enumerate(PHASES)}
    pending = []

    d = lax.axis_index("dp")
    z = lax.axis_index("col")
    c = d % 2
    x = (d // 2) % NX
    y = d // 8
    oc = 1 - c
    worker = y < NM

    def dev(yy, xx, cc, zz):
        return ((yy * NX + xx) * 2 + cc, zz)

    sib = dev(y, x, oc, z)

    def xpeer(k):
        return dev(y, (x + k) % NX, c, z)

    def ypeer(k):
        return dev((y + k) % NY, x, c, z)

    def zpeer(k):
        return dev(y, x, c, (z + k) % NZ)

    def remote(phase, src, dst, to, send=0, recv=0):
        return pltpu.make_async_remote_copy(
            src_ref=src,
            dst_ref=dst,
            send_sem=S[phase][0].at[send],
            recv_sem=S[phase][1].at[recv],
            device_id=to,
            device_id_type=pl.DeviceIdType.MESH,
        )

    def received(phase, ref, recv=0):
        remote(phase, ref, ref, sib, recv=recv).wait_recv()

    def sent(phase, ref, send=0):
        remote(phase, ref, ref, sib, send=send).wait_send()

    def local(i, src, dst):
        return pltpu.make_async_copy(src, dst, S["loc"][0].at[i])

    def cols(cc):
        return pl.ds(pl.multiple_of(cc * 128, 128), 128)

    def rows8(cc):
        return pl.ds(pl.multiple_of(cc * 8, 8), 8)

    def rows16(at):
        return pl.ds(pl.multiple_of(at * 16, 16), 16)

    def flush():
        for wait in pending:
            wait()
        pending.clear()

    loc = [
        local(0, g.at[:, :, cols(c)], B["own_g"]),
        local(1, mom.at[:, :, cols(c)], B["mom16"].at[:, rows8(c), :]),
        local(2, mas.at[:, :, cols(c)], B["mas16"].at[:, rows8(c), :]),
        local(3, mas, B["mas"]),
    ]
    for item in loc:
        item.start()

    barrier = pltpu.get_barrier_semaphore()
    partners = [sib] + [xpeer(k) for k in range(1, NX)]
    partners += [ypeer(k) for k in range(1, NY)] + [zpeer(k) for k in range(1, NZ)]
    for to in partners:
        pl.semaphore_signal(barrier, inc=1, device_id=to, device_id_type=pl.DeviceIdType.MESH)
    pl.semaphore_wait(barrier, len(partners))
    yield "barrier", flush

    sg = {
        m: remote("sg", g.at[m, :, cols(oc)], B["sib_g"].at[m], sib, send=m, recv=m) for m in ORDER
    }
    smo = remote("smo", mom.at[:, :, cols(oc)], B["mom16"].at[:, rows8(c), :], sib)
    sma = remote("sma", mas.at[:, :, cols(oc)], B["mas16"].at[:, rows8(c), :], sib)
    for m in ORDER:
        sg[m].start()
    smo.start()
    sma.start()
    pending += [sg[m].wait_send for m in ORDER] + [smo.wait_send, sma.wait_send]
    for item in loc:
        item.wait()

    for m in ORDER:
        sg[m].wait_recv()

        def add_pair(xx, carry, m=m):
            for yy in range(NY):
                rows = rows16(yy * 4 + xx)
                total = B["own_g"][m, rows, :].astype(f32) + B["sib_g"][m, rows, :].astype(f32)
                B["sum1"][m, xx, pl.ds(yy * 16, 16), :] = total.astype(bf16)
            return carry

        lax.fori_loop(0, NX, add_pair, 0)
        for k in (2, 1, 3):
            remote(
                "x1", B["sum1"].at[m, (x + k) % NX], B["xr"].at[m, k - 1], xpeer(k), recv=m
            ).start()
    pending.append(lambda: sent("x1", B["xr"]))
    yield "pair", flush

    smo.wait_recv()
    sma.wait_recv()

    def my(m):
        slot = (m - y + NY) % NY - 1
        return remote("my", B["mom16"].at[m], B["momr"].at[y], dev(m, x, c, z), send=slot)

    def y1(m):
        slot = (m - y + NY) % NY - 1
        return remote("y1", B["sum2"].at[m], B["yr"].at[slot], dev(m, x, c, z), send=slot)

    def not_mine(op, m):
        @pl.when(y != m)
        def _():
            op(m)

    for m in ORDER:
        not_mine(lambda m: my(m).start(), m)

        @pl.when(y == m)
        def _(m=m):
            B["momr"][m] = B["mom16"][m]

    B["masb"][...] = B["mas16"][...].astype(bf16)

    for m in ORDER:
        received("x1", B["xr"].at[m], recv=m)
        total = B["sum1"][m, x].astype(f32)
        for k in range(1, NX):
            total = total + B["xr"][m, k - 1].astype(f32)
        B["sum2"][m] = total.astype(bf16)
        not_mine(lambda m: y1(m).start(), m)

    for m in ORDER:
        pending.append(lambda m=m: not_mine(lambda m: my(m).wait_send(), m))
        pending.append(lambda m=m: not_mine(lambda m: y1(m).wait_send(), m))
    yield "x", flush

    for k in range(1, NY):
        remote("ay", B["masb"], B["mb"].at[c, x, y], ypeer(k)).start()
    B["mb"][c, x, y] = B["masb"][...]
    pending.append(lambda: sent("ay", B["mb"].at[c, x, pl.ds(0, NY - 1)]))

    def dot(left, right):
        return jnp.dot(left, right, preferred_element_type=f32)

    def ny(yy):
        return remote(
            "ny", B["nmw"].at[yy], B["nm16"].at[y], dev(yy, x, c, z), send=yy, recv=y
        )

    @pl.when(worker)
    def _():
        received("my", B["momr"].at[pl.ds(0, NY - 1)])
        received("y1", B["yr"])
        summed = B["sum2"][y].astype(f32)
        for k in range(1, NY):
            summed = summed + B["yr"][k - 1].astype(f32)
        new_mom = momentum_decay * B["momr"][...].reshape(128, 128) + summed
        B["u"][x] = (summed + momentum_decay * new_mom).astype(bf16)
        for k in (2, 1, 3):
            remote("ux", B["u"].at[x], B["u"].at[x], xpeer(k)).start()
        B["nmw"][...] = new_mom.reshape(NY, 16, 128)
        B["nm16"][y] = B["nmw"][y]
    yield "y", flush

    @pl.when(worker)
    def _():
        received("ux", B["u"].at[pl.ds(0, NX - 1)])
    yield "ux", flush

    @pl.when(worker)
    def _():
        B["part"][...] = lax.dot_general(
            B["u"][x], B["u"][...].reshape(KV, 128), (((1,), (1,)), ((), ())),
            preferred_element_type=f32,
        )
        B["gps"][...] = B["part"][pl.ds(pl.multiple_of(oc * 64, 64), 64), :].astype(bf16)
        gs = remote("gs", B["gps"], B["gpr"], sib)
        gs.start()
        gs.wait_recv()
        mine = B["part"][pl.ds(pl.multiple_of(c * 64, 64), 64), :] + B["gpr"][...].astype(f32)
        for p in range(NZ):
            at, to = (p // 2) * 16, (p % 2) * 256
            B["gzs"][p] = mine[at:at + 16, to:to + 256].astype(bf16)
        for k in (4, 3, 5, 2, 6, 1, 7):
            remote("zr", B["gzs"].at[(z + k) % NZ], B["gzr"].at[k - 1], zpeer(k)).start()
        for yy in range(NY):
            @pl.when(y != yy)
            def _(yy=yy):
                ny(yy).start()
    yield "gs", flush

    received("ay", B["mb"].at[c, x, pl.ds(0, NY - 1)])
    for k in range(1, NX):
        remote("ax", B["mb"].at[c, x], B["mb"].at[c, x], xpeer(k)).start()
    flush()
    pending.append(lambda: sent("ax", B["mb"].at[c, pl.ds(0, NX - 1)]))

    def drain_head():
        sent("ux", B["u"].at[pl.ds(0, NX - 1)])
        sent("gs", B["gps"])
        sent("zr", B["gzr"])
        for yy in range(NY):
            @pl.when(y != yy)
            def _(yy=yy):
                ny(yy).wait_send()

    pending.append(lambda: pl.when(worker)(drain_head))

    @pl.when(worker)
    def _():
        received("zr", B["gzr"])
        total = B["gzs"][z].astype(f32)
        for k in range(1, NZ):
            total = total + B["gzr"][k - 1].astype(f32)
        B["gz"][z] = total.astype(bf16)
        for k in (4, 3, 5, 2, 6, 1, 7):
            remote("za", B["gz"].at[z], B["gz"].at[z], zpeer(k)).start()
    pending.append(lambda: pl.when(worker)(lambda: sent("za", B["gz"].at[pl.ds(0, NZ - 1)])))
    yield "zr", flush

    @pl.when(worker)
    def _():
        received("za", B["gz"].at[pl.ds(0, NZ - 1)])
        for p in range(NZ):
            at, to = (p // 2) * 16, (p % 2) * 256
            B["g4"][c, x, at:at + 16, to:to + 256] = B["gz"][p]
        for k in (2, 1, 3):
            remote("gx", B["g4"].at[c, x], B["g4"].at[c, x], xpeer(k)).start()
    pending.append(lambda: pl.when(worker)(lambda: sent("gx", B["g4"].at[c, pl.ds(0, NX - 1)])))
    yield "za", flush

    @pl.when(worker)
    def _():
        received("gx", B["g4"].at[c, pl.ds(0, NX - 1)])
        gc = remote("gc", B["g4"].at[c], B["g4"].at[c], sib)
        gc.start()
        gc.wait_recv()
    pending.append(lambda: pl.when(worker)(lambda: sent("gc", B["g4"].at[c])))
    yield "gx", flush

    received("ax", B["mb"].at[c, pl.ds(0, NX - 1)])
    ac = remote("ac", B["mb"].at[c], B["mb"].at[c], sib)
    ac.start()
    pending.append(ac.wait_send)

    def sq(yy):
        return remote("sq", B["sqw"], B["sqr"].at[y], dev(yy, x, c, z), send=yy, recv=y)

    @pl.when(worker)
    def _():
        for xx in range(NX):
            for cc in range(2):
                at = (xx * 2 + cc) * 64
                B["gf"][at:at + 64, :] = B["g4"][cc, xx].astype(f32)
        gram = B["gf"][...]
        diagonal = lax.broadcasted_iota(jnp.int32, (512, 512), 0) == lax.broadcasted_iota(
            jnp.int32, (512, 512), 1
        )
        squares = jnp.sum(
            jnp.sum(jnp.where(diagonal, gram, 0.0), axis=0, keepdims=True), axis=1, keepdims=True
        )
        B["sqw"][...] = jnp.broadcast_to(squares, (8, 128))
        for yy in range(NY):
            @pl.when(y != yy)
            def _(yy=yy):
                sq(yy).start()
        B["sqr"][y] = B["sqw"][...]
        scale = 1.0 / (jnp.sqrt(squares) + epsilon)
        gram = (gram * scale) * scale

        def mixing(gram, half):
            return (quintic_second * gram + quintic_third * dot(half, half)).astype(bf16)

        def advance(gram, half, mix):
            once = quintic_first * gram + dot(mix, half)
            return quintic_first * once + dot(once.astype(bf16), mix)

        B["gb"][...] = gram.astype(bf16)
        B["m0"][...] = mixing(gram, B["gb"][...])
        gram = advance(gram, B["gb"][...], B["m0"][...])
        B["gb"][...] = gram.astype(bf16)
        B["m1"][...] = mixing(gram, B["gb"][...])
        gram = advance(gram, B["gb"][...], B["m1"][...])
        B["gf"][...] = gram
        B["gb"][...] = gram.astype(bf16)
        mine = pl.ds(pl.multiple_of(x * 128, 128), 128)
        mix2 = (
            quintic_second * B["gf"][mine, :]
            + quintic_third * dot(B["gb"][mine, :], B["gb"][...])
        ).astype(bf16)
        k1 = quintic_first * (B["m1"][mine, :].astype(f32) + mix2.astype(f32)) + dot(
            mix2, B["m1"][...]
        )
        k0 = (
            quintic_first**2 * B["m0"][mine, :].astype(f32)
            + quintic_first * k1
            + dot(k1.astype(bf16), B["m0"][...])
        )
        last = quintic_first**3 * B["u"][x].astype(f32) + dot(
            k0.astype(bf16), B["u"][...].reshape(KV, 128)
        )
        last = (last * scale).astype(bf16)
        B["big"][c, y, x] = (factor * last.astype(f32)).astype(bf16)
    yield "ns", flush

    @pl.when(worker)
    def _():
        for k in (4, 3, 5, 2, 6, 1, 7):
            remote("sy", B["big"].at[c, y, x], B["big"].at[c, y, x], ypeer(k), recv=y).start()

    def drain_worker():
        sent("sy", B["yr"])
        for yy in range(NY):
            @pl.when(y != yy)
            def _(yy=yy):
                sq(yy).wait_send()

    for m in range(NM):
        not_mine(lambda m: received("ny", B["nm16"].at[m], recv=m), m)
    ns = remote("ns", B["nm16"].at[:, rows8(oc), :], B["nmsib"], sib)
    ns.start()
    pending.append(ns.wait_send)
    nm_out[:, :, cols(c)] = B["nm16"][:, rows8(c), :]
    ac.wait_recv()
    flush()
    ns.wait_recv()
    nm_out[:, :, cols(oc)] = B["nmsib"][...]

    for m in ORDER:
        not_mine(lambda m: received("sy", B["big"].at[c, m, x], recv=m), m)
        for k in (2, 1, 3):
            remote("sx", B["big"].at[c, m, x], B["big"].at[c, m, x], xpeer(k), recv=m).start()
    pending.append(lambda: pl.when(worker)(drain_worker))
    pending.append(lambda: sent("sx", B["xr"]))
    yield "sy", flush

    ids = [owners[m] for m in range(NM)]
    slots = [sum([(ids[j] == ids[m]).astype(jnp.int32) for j in range(m)], jnp.int32(0)) for m in range(NM)]
    picks = [[(ids[m] == d) & (slots[m] == s) for m in range(NM)] for s in range(MOST)]

    def finish(cc, m, first):
        def one(xx, carry):
            for yy in range(NY):
                rows = rows16(yy * 4 + xx)
                scaled = B["big"][cc, m, xx, pl.ds(yy * 16, 16), :]
                master = B["mb"][cc, xx, yy, m].astype(f32)
                B["w"][m, rows, cols(cc)] = (
                    master * (1.0 - learn_rate * weight_decay) - learn_rate * scaled.astype(f32)
                ).astype(bf16)
                for s in range(MOST):
                    before = jnp.zeros_like(scaled) if first else B["ow"][s, rows, cols(cc)]
                    B["ow"][s, rows, cols(cc)] = jnp.where(picks[s][m], scaled, before)
            return carry

        lax.fori_loop(0, NX, one, 0)
        own = B["big"][cc, m, x, pl.ds(pl.multiple_of(y * 16, 16), 16), :].astype(f32)
        own = jnp.where(c == 0, own[0:8], own[8:16])
        ma_out[m, :, cols(cc)] = (
            B["mas"][m, :, cols(cc)] * (1.0 - learn_rate * weight_decay) - learn_rate * own
        )

    for m in ORDER:
        received("sx", B["big"].at[c, m, pl.ds(0, NX - 1)], recv=m)
        remote("sc", B["big"].at[c, m], B["big"].at[c, m], sib, recv=m).start()
        finish(c, m, m == ORDER[0])
    pending.append(lambda: sent("sc", B["big"].at[c]))
    yield "sx", flush

    for m in range(NM):
        not_mine(lambda m: received("sq", B["sqr"].at[m], recv=m), m)
    lane = lax.broadcasted_iota(jnp.int32, (1, 128), 1)
    rms = jnp.zeros((1, 128), f32)
    for m in range(NM):
        value = jnp.sqrt(B["sqr"][m, 0:1, :] / float(KV * D))
        for s in range(MOST):
            rms = rms + jnp.where(picks[s][m] & (lane == s), value, 0.0)
    rms_out[...] = rms[:, 0:MOST]
    done = []
    for m in ORDER:
        received("sc", B["big"].at[oc, m], recv=m)
        finish(oc, m, m == ORDER[0])
        pltpu.make_async_copy(B["w"].at[m], w_out.at[m], S["out"][0].at[0]).start()
    out = pltpu.make_async_copy(B["ow"], ow_out, S["out"][1].at[0])
    out.start()
    flush()
    pltpu.make_async_copy(B["w"], w_out, S["out"][0].at[0]).wait()
    out.wait()


def kernel(stop, *refs):
    for name, flush in stages(*refs):
        if name == stop:
            flush()
            break


def step(owners, g, mom, mas, stop=None, collective_id=0):
    vmem = pl.BlockSpec(memory_space=pltpu.VMEM)
    anywhere = pl.BlockSpec(memory_space=pl.ANY)
    scratch = [pltpu.VMEM(*spec) for spec in BUFFERS.values()]
    for send, recv in PHASES.values():
        scratch += [pltpu.SemaphoreType.DMA((send,)), pltpu.SemaphoreType.DMA((recv,))]
    return pl.pallas_call(
        functools.partial(kernel, stop),
        out_shape=(
            jax.ShapeDtypeStruct((NM, KV, 256), bf16),
            jax.ShapeDtypeStruct((NM, 8, 256), f32),
            jax.ShapeDtypeStruct((NM, 8, 256), f32),
            jax.ShapeDtypeStruct((MOST, KV, 256), bf16),
            jax.ShapeDtypeStruct((1, MOST), f32),
        ),
        in_specs=[pl.BlockSpec(memory_space=pltpu.SMEM), anywhere, anywhere, anywhere],
        out_specs=(anywhere, vmem, vmem, anywhere, vmem),
        scratch_shapes=scratch,
        compiler_params=pltpu.CompilerParams(
            collective_id=collective_id, has_side_effects=True, vmem_limit_bytes=60 * 1024 * 1024
        ),
        name="muon_step",
    )(owners, g, mom, mas)


def per_device(gradients, momentum, master, owners):
    new_weights, new_momentum, new_master, owned_updates, owned_rms = step(
        owners, gradients[0], momentum, master
    )
    return (new_weights, new_master, new_momentum, owned_updates[None], owned_rms)


def solution(mesh):
    return jax.shard_map(
        per_device,
        mesh=mesh,
        in_specs=(P("dp", None, None, "col"), P(None, "dp", "col"), P(None, "dp", "col"), P()),
        out_specs=(
            P(None, None, "col"),
            P(None, "dp", "col"),
            P(None, "dp", "col"),
            P("dp", None, None, "col"),
            P("dp", None),
        ),
        check_vma=False,
    )
```

time: 575 us -> 80.6 us (0.14)
  waiting for transfers between devices: 459 us -> 0 us
  blocking collectives: 76.7 us -> 0 us
  Pallas kernels: 0 us -> 73.4 us
  matrix products: 14.1 us -> 0 us
  between operations: 13.9 us -> 0.68 us
  other arithmetic: 6.4 us -> 0 us
    psum x3 -> x0, waiting for transfers between devices: 236 us -> none  [newton(): lax.psum(partial_value.astype(jnp.bfloat16), 'col').astype(jnp.float32)]
    reduce_scatter x1 -> x0, waiting for transfers between devices: 152 us -> none  [per_device(): summed = lax.psum_scatter(terms, 'dp', scatter_dimension=1, tiled=True)]
    pallas_call x0 -> x1, Pallas kernels: none -> 73.4 us  [step(): pl.pallas_call(functools.partial(kernel, stop), out_shape=(jax.ShapeDtype...]
    all_gather x1 -> x0, waiting for transfers between devices: 70.6 us -> none  [per_device(): lax.all_gather(new_master.astype(jnp.bfloat16), 'dp', axis=1, tiled=True)]
    all_to_all x2 -> x0, blocking collectives: 62.2 us -> none  [the longest x1 31.8 us: per_device(): lax.all_to_all(owned_updates, 'dp', split_axis=2, concat_axis=0, tiled=True)]
    psum x1 -> x0, blocking collectives: 14.5 us -> none  [newton(): squares = lax.psum(local_sum, 'col')]
    dot_general x8 -> x0, matrix products: 14.1 us -> none  [the longest x3 9.15 us: newton(): jnp.einsum('sij,sjk->sik', mixing, iterate, preferred_element_type=jnp.fl...]
  transfers between devices with their start and end apart: 5 -> 0, of which waited for: 5 -> 0; matrix products, arithmetic and copies ran while one was open for 0% -> 0% of each run, Pallas kernels for 0% -> 0%
where the time goes in v2:
time: 80.6 us; the launch traced here: 79.4 us
  Pallas kernels  73.4 us (91%)
  local copies, waits for them, and re-layouts  5.27 us (7%)
    pallas_call x1, Pallas kernels, step(): pl.pallas_call(functools.partial(kernel, stop), out_shape=(jax.ShapeDtype...  73.4 us
    unnamed x13, local copies, waits for them, and re-layouts  5.27 us

profile of v2, /device:TPU:1, one launch (start us, length us, event | category | flops | bytes accessed | tf_op | source)
XLA Modules:
  0.0 79.4 jit_solution(10015257163472273676)
XLA Ops:
  0.6 73.4 %muon_step.1 = (bf16[6,512,256]{2,1,0:T(8,128)(2,1)}, f32[6,8,256]{2,1,0:T(8,128)}, f32[6,8,256]{2,1,0:T(8,128)}, bf16[2,512,256]{2,1,0:T(8,128)(2,1)}, f32[1,2]{1,0:T(1,128)}) custom-call(s32[6]{0:T(128)} %refs_0_.1, bf16[6,512,256]{2,1,0:T(8,128)(2,1)} %bitcast.2, f32[6,8,256]{2,1,0:T(8,128)} %refs_2_.1, f32[6,8,256]{2,1,0:T(8,128)} %refs_3_.1), custom_call_target="tpu_custom_call" | custom-call | tf_op jit(solution)/shard_map/muon_step/pallas_call | solution.py:487
  74.1 0.0 copy-start.2
  74.1 0.0 copy-start.1
  74.1 0.0 copy-start
  74.1 0.0 copy-start.3
  74.1 2.7 %copy.14 = bf16[6,512,256]{2,1,0:T(8,128)(2,1)} copy(bf16[6,512,256]{2,1,0:T(8,128)(2,1)} %get-tuple-element.20) | data formatting | bytes 3145728
  76.8 0.0 copy-done.2
  76.8 0.6 copy.15
  77.4 0.0 copy-done.1
  77.4 0.6 copy.16
  78.1 0.0 copy-done
  78.1 0.8 copy.17
  78.9 0.0 copy-done.3
  78.9 0.5 copy.18
Async XLA Ops:
  74.1 2.8 %copy-start.2 = (f32[6,8,256]{2,1,0:T(8,128)S(1)}, f32[6,8,256]{2,1,0:T(8,128)}, u32[]{:S(2)}) copy-start(f32[6,8,256]{2,1,0:T(8,128)} %get-tuple-element.21) | copy-start | bytes 147460
  74.1 3.4 %copy-start.1 = (f32[6,8,256]{2,1,0:T(8,128)S(1)}, f32[6,8,256]{2,1,0:T(8,128)}, u32[]{:S(2)}) copy-start(f32[6,8,256]{2,1,0:T(8,128)} %get-tuple-element.22) | copy-start | bytes 147460
  74.1 4.0 %copy-start = (bf16[2,512,256]{2,1,0:T(8,128)(2,1)S(1)}, bf16[2,512,256]{2,1,0:T(8,128)(2,1)}, u32[]{:S(2)}) copy-start(bf16[2,512,256]{2,1,0:T(8,128)(2,1)} %get-tuple-element.13) | copy-start | bytes 1572868
  74.1 4.8 %copy-start.3 = (f32[1,2]{1,0:T(1,128)S(1)}, f32[1,2]{1,0:T(1,128)}, u32[]{:S(2)}) copy-start(f32[1,2]{1,0:T(1,128)} %get-tuple-element.24) | copy-start | bytes 28

commit v3 on v2

--- a/solution.py
+++ b/solution.py
@@ -27,7 +27,8 @@
 
 f32 = jnp.float32
 bf16 = jnp.bfloat16
-ORDER = (0, 3, 1, 4, 2, 5)
+FAR = (4, 3, 5, 2, 6, 1, 7, 0)
+NEAR = (0, 1, 7, 2, 6, 3, 5, 4)
 
 BUFFERS = dict(
     own_g=((NM, KV, 128), bf16),
@@ -60,11 +61,9 @@
     sqr=((NM, 8, 128), f32),
     big=((2, NM, NX, 128, 128), bf16),
     mb=((2, NX, NY, NM, 16, 128), bf16),
-    w=((NM, KV, 256), bf16),
-    ow=((MOST, KV, 256), bf16),
 )
 PHASES = dict(
-    loc=(4, 1), out=(1, 1), sg=(NM, NM), smo=(1, 1), sma=(1, 1), x1=(1, NM), y1=(7, 1), my=(7, 1),
+    loc=(4, 1), sg=(1, NM), smo=(1, 1), sma=(1, 1), x1=(1, NM), y1=(7, 1), my=(7, 1),
     ay=(1, 1), ux=(1, 1), gs=(1, 1), zr=(1, 1), za=(1, 1), gx=(1, 1), gc=(1, 1), ax=(1, 1),
     ac=(1, 1), ny=(8, NM), ns=(1, 1), sq=(8, NM), sy=(1, NM), sx=(1, NM), sc=(1, NM),
 )
@@ -147,36 +146,44 @@
     for to in partners:
         pl.semaphore_signal(barrier, inc=1, device_id=to, device_id_type=pl.DeviceIdType.MESH)
     pl.semaphore_wait(barrier, len(partners))
+    ow_out[...] = jnp.zeros_like(ow_out)
     yield "barrier", flush
 
-    sg = {
-        m: remote("sg", g.at[m, :, cols(oc)], B["sib_g"].at[m], sib, send=m, recv=m) for m in ORDER
-    }
+    def each(order, op):
+        for delta in order:
+            m = (y + delta) % NY
+            pl.when(m < NM)(functools.partial(op, m, delta))
+
     smo = remote("smo", mom.at[:, :, cols(oc)], B["mom16"].at[:, rows8(c), :], sib)
     sma = remote("sma", mas.at[:, :, cols(oc)], B["mas16"].at[:, rows8(c), :], sib)
-    for m in ORDER:
-        sg[m].start()
     smo.start()
     sma.start()
-    pending += [sg[m].wait_send for m in ORDER] + [smo.wait_send, sma.wait_send]
+
+    def swap(m, delta):
+        remote("sg", g.at[m, :, cols(oc)], B["sib_g"].at[m], sib, recv=m).start()
+
+    each(FAR, swap)
+    pending += [lambda: sent("sg", B["sib_g"]), smo.wait_send, sma.wait_send]
     for item in loc:
         item.wait()
 
-    for m in ORDER:
-        sg[m].wait_recv()
-
-        def add_pair(xx, carry, m=m):
+    def pair(m, delta):
+        received("sg", B["sib_g"].at[m], recv=m)
+
+        def add(xx, carry):
             for yy in range(NY):
                 rows = rows16(yy * 4 + xx)
                 total = B["own_g"][m, rows, :].astype(f32) + B["sib_g"][m, rows, :].astype(f32)
                 B["sum1"][m, xx, pl.ds(yy * 16, 16), :] = total.astype(bf16)
             return carry
 
-        lax.fori_loop(0, NX, add_pair, 0)
+        lax.fori_loop(0, NX, add, 0)
         for k in (2, 1, 3):
             remote(
                 "x1", B["sum1"].at[m, (x + k) % NX], B["xr"].at[m, k - 1], xpeer(k), recv=m
             ).start()
+
+    each(FAR, pair)
     pending.append(lambda: sent("x1", B["xr"]))
     yield "pair", flush
 
@@ -196,7 +203,7 @@
         def _():
             op(m)
 
-    for m in ORDER:
+    for m in range(NM):
         not_mine(lambda m: my(m).start(), m)
 
         @pl.when(y == m)
@@ -204,24 +211,25 @@
             B["momr"][m] = B["mom16"][m]
 
     B["masb"][...] = B["mas16"][...].astype(bf16)
-
-    for m in ORDER:
+    for k in (4, 3, 5, 2, 6, 1, 7):
+        remote("ay", B["masb"], B["mb"].at[c, x, y], ypeer(k)).start()
+    B["mb"][c, x, y] = B["masb"][...]
+    pending.append(lambda: sent("ay", B["mb"].at[c, x, pl.ds(0, NY - 1)]))
+
+    def along_x(m, delta):
         received("x1", B["xr"].at[m], recv=m)
         total = B["sum1"][m, x].astype(f32)
         for k in range(1, NX):
             total = total + B["xr"][m, k - 1].astype(f32)
         B["sum2"][m] = total.astype(bf16)
-        not_mine(lambda m: y1(m).start(), m)
-
-    for m in ORDER:
+        if delta:
+            y1(m).start()
+
+    each(FAR, along_x)
+    for m in range(NM):
         pending.append(lambda m=m: not_mine(lambda m: my(m).wait_send(), m))
         pending.append(lambda m=m: not_mine(lambda m: y1(m).wait_send(), m))
     yield "x", flush
-
-    for k in range(1, NY):
-        remote("ay", B["masb"], B["mb"].at[c, x, y], ypeer(k)).start()
-    B["mb"][c, x, y] = B["masb"][...]
-    pending.append(lambda: sent("ay", B["mb"].at[c, x, pl.ds(0, NY - 1)]))
 
     def dot(left, right):
         return jnp.dot(left, right, preferred_element_type=f32)
@@ -332,17 +340,14 @@
 
     @pl.when(worker)
     def _():
+        row = lax.broadcasted_iota(jnp.int32, (64, 128), 0)
+        col = lax.broadcasted_iota(jnp.int32, (64, 128), 1)
+        squares = jnp.zeros((64, 128), f32)
         for xx in range(NX):
             for cc in range(2):
-                at = (xx * 2 + cc) * 64
-                B["gf"][at:at + 64, :] = B["g4"][cc, xx].astype(f32)
-        gram = B["gf"][...]
-        diagonal = lax.broadcasted_iota(jnp.int32, (512, 512), 0) == lax.broadcasted_iota(
-            jnp.int32, (512, 512), 1
-        )
-        squares = jnp.sum(
-            jnp.sum(jnp.where(diagonal, gram, 0.0), axis=0, keepdims=True), axis=1, keepdims=True
-        )
+                block = B["g4"][cc, xx, :, xx * 128:xx * 128 + 128].astype(f32)
+                squares = squares + jnp.where(row + cc * 64 == col, block, 0.0)
+        squares = jnp.sum(jnp.sum(squares, axis=0, keepdims=True), axis=1, keepdims=True)
         B["sqw"][...] = jnp.broadcast_to(squares, (8, 128))
         for yy in range(NY):
             @pl.when(y != yy)
@@ -350,7 +355,11 @@
                 sq(yy).start()
         B["sqr"][y] = B["sqw"][...]
         scale = 1.0 / (jnp.sqrt(squares) + epsilon)
-        gram = (gram * scale) * scale
+        for xx in range(NX):
+            for cc in range(2):
+                at = (xx * 2 + cc) * 64
+                B["gf"][at:at + 64, :] = (B["g4"][cc, xx].astype(f32) * scale) * scale
+        gram = B["gf"][...]
 
         def mixing(gram, half):
             return (quintic_second * gram + quintic_third * dot(half, half)).astype(bf16)
@@ -410,30 +419,39 @@
     ns.wait_recv()
     nm_out[:, :, cols(oc)] = B["nmsib"][...]
 
-    for m in ORDER:
-        not_mine(lambda m: received("sy", B["big"].at[c, m, x], recv=m), m)
+    def on_x(m, delta):
+        if delta:
+            received("sy", B["big"].at[c, m, x], recv=m)
         for k in (2, 1, 3):
             remote("sx", B["big"].at[c, m, x], B["big"].at[c, m, x], xpeer(k), recv=m).start()
+
+    each(NEAR, on_x)
     pending.append(lambda: pl.when(worker)(drain_worker))
     pending.append(lambda: sent("sx", B["xr"]))
     yield "sy", flush
 
-    ids = [owners[m] for m in range(NM)]
-    slots = [sum([(ids[j] == ids[m]).astype(jnp.int32) for j in range(m)], jnp.int32(0)) for m in range(NM)]
-    picks = [[(ids[m] == d) & (slots[m] == s) for m in range(NM)] for s in range(MOST)]
-
-    def finish(cc, m, first):
+    def picks(m):
+        mine = owners[m]
+        slot = jnp.int32(0)
+        for j in range(NM):
+            slot = slot + ((owners[j] == mine) & (j < m)).astype(jnp.int32)
+        return [(mine == d) & (slot == s) for s in range(MOST)]
+
+    def finish(cc, m):
+        chosen = picks(m)
+
         def one(xx, carry):
             for yy in range(NY):
                 rows = rows16(yy * 4 + xx)
                 scaled = B["big"][cc, m, xx, pl.ds(yy * 16, 16), :]
                 master = B["mb"][cc, xx, yy, m].astype(f32)
-                B["w"][m, rows, cols(cc)] = (
+                w_out[m, rows, cols(cc)] = (
                     master * (1.0 - learn_rate * weight_decay) - learn_rate * scaled.astype(f32)
                 ).astype(bf16)
                 for s in range(MOST):
-                    before = jnp.zeros_like(scaled) if first else B["ow"][s, rows, cols(cc)]
-                    B["ow"][s, rows, cols(cc)] = jnp.where(picks[s][m], scaled, before)
+                    ow_out[s, rows, cols(cc)] = jnp.where(
+                        chosen[s], scaled, ow_out[s, rows, cols(cc)]
+                    )
             return carry
 
         lax.fori_loop(0, NX, one, 0)
@@ -443,10 +461,12 @@
             B["mas"][m, :, cols(cc)] * (1.0 - learn_rate * weight_decay) - learn_rate * own
         )
 
-    for m in ORDER:
+    def to_sibling(m, delta):
         received("sx", B["big"].at[c, m, pl.ds(0, NX - 1)], recv=m)
         remote("sc", B["big"].at[c, m], B["big"].at[c, m], sib, recv=m).start()
-        finish(c, m, m == ORDER[0])
+        finish(c, m)
+
+    each(NEAR, to_sibling)
     pending.append(lambda: sent("sc", B["big"].at[c]))
     yield "sx", flush
 
@@ -456,19 +476,17 @@
     rms = jnp.zeros((1, 128), f32)
     for m in range(NM):
         value = jnp.sqrt(B["sqr"][m, 0:1, :] / float(KV * D))
+        chosen = picks(m)
         for s in range(MOST):
-            rms = rms + jnp.where(picks[s][m] & (lane == s), value, 0.0)
+            rms = rms + jnp.where(chosen[s] & (lane == s), value, 0.0)
     rms_out[...] = rms[:, 0:MOST]
-    done = []
-    for m in ORDER:
+
+    def from_sibling(m, delta):
         received("sc", B["big"].at[oc, m], recv=m)
-        finish(oc, m, m == ORDER[0])
-        pltpu.make_async_copy(B["w"].at[m], w_out.at[m], S["out"][0].at[0]).start()
-    out = pltpu.make_async_copy(B["ow"], ow_out, S["out"][1].at[0])
-    out.start()
+        finish(oc, m)
+
+    each(NEAR, from_sibling)
     flush()
-    pltpu.make_async_copy(B["w"], w_out, S["out"][0].at[0]).wait()
-    out.wait()
 
 
 def kernel(stop, *refs):
@@ -480,32 +498,54 @@
 
 def step(owners, g, mom, mas, stop=None, collective_id=0):
     vmem = pl.BlockSpec(memory_space=pltpu.VMEM)
-    anywhere = pl.BlockSpec(memory_space=pl.ANY)
+    hbm = pl.BlockSpec(memory_space=pltpu.HBM)
     scratch = [pltpu.VMEM(*spec) for spec in BUFFERS.values()]
     for send, recv in PHASES.values():
         scratch += [pltpu.SemaphoreType.DMA((send,)), pltpu.SemaphoreType.DMA((recv,))]
     return pl.pallas_call(
         functools.partial(kernel, stop),
         out_shape=(
-            jax.ShapeDtypeStruct((NM, KV, 256), bf16),
-            jax.ShapeDtypeStruct((NM, 8, 256), f32),
-            jax.ShapeDtypeStruct((NM, 8, 256), f32),
-            jax.ShapeDtypeStruct((MOST, KV, 256), bf16),
-            jax.ShapeDtypeStruct((1, MOST), f32),
+            pltpu.VMEM((NM, KV, 256), bf16),
+            pltpu.VMEM((NM, 8, 256), f32),
+            pltpu.VMEM((NM, 8, 256), f32),
+            pltpu.VMEM((MOST, KV, 256), bf16),
+            pltpu.VMEM((1, MOST), f32),
         ),
-        in_specs=[pl.BlockSpec(memory_space=pltpu.SMEM), anywhere, anywhere, anywhere],
-        out_specs=(anywhere, vmem, vmem, anywhere, vmem),
+        in_specs=[pl.BlockSpec(memory_space=pltpu.SMEM), hbm, hbm, hbm],
+        out_specs=(vmem, vmem, vmem, vmem, vmem),
         scratch_shapes=scratch,
         compiler_params=pltpu.CompilerParams(
-            collective_id=collective_id, has_side_effects=True, vmem_limit_bytes=60 * 1024 * 1024
+            collective_id=collective_id, has_side_effects=True, vmem_limit_bytes=40 * 1024 * 1024
         ),
         name="muon_step",
-    )(owners, g, mom, mas)
+    )(*(pltpu.with_memory_space_constraint(item, pltpu.HBM) for item in (owners, g, mom, mas)))
+
+
+def copy_kernel(*refs):
+    count = (len(refs) - 1) // 2
+    copies = [
+        pltpu.make_async_copy(refs[i], refs[count + i], refs[-1].at[i]) for i in range(count)
+    ]
+    for copy in copies:
+        copy.start()
+    for copy in copies:
+        copy.wait()
+
+
+def write_out(arrays):
+    return pl.pallas_call(
+        copy_kernel,
+        out_shape=[jax.ShapeDtypeStruct(item.shape, item.dtype) for item in arrays],
+        in_specs=[pl.BlockSpec(memory_space=pl.ANY)] * len(arrays),
+        out_specs=[pl.BlockSpec(memory_space=pl.ANY)] * len(arrays),
+        scratch_shapes=[pltpu.SemaphoreType.DMA((len(arrays),))],
+        name="write_out",
+    )(*(pltpu.with_memory_space_constraint(item, pltpu.VMEM) for item in arrays))
 
 
 def per_device(gradients, momentum, master, owners):
-    new_weights, new_momentum, new_master, owned_updates, owned_rms = step(
-        owners, gradients[0], momentum, master
+    new_weights, new_momentum, new_master, owned_updates, owned_rms = write_out(
+        step(owners, gradients[0], momentum, master)
     )
     return (new_weights, new_master, new_momentum, owned_updates[None], owned_rms)
 

time: 80.6 us -> 75.2 us (0.933)
  the two profiles are of different devices: /device:TPU:1 before, /device:TPU:57 now
where the time goes in v3:
time: 75.2 us; the launch traced here: 75.1 us
  Pallas kernels  74.4 us (99%)
    pallas_call x1, Pallas kernels, step(): pl.pallas_call(functools.partial(kernel, stop), out_shape=(pltpu.VMEM((NM...  73 us

profile of v3, /device:TPU:57, one launch (start us, length us, event | category | flops | bytes accessed | tf_op | source)
XLA Modules:
  0.0 75.1 jit_solution(17215674728703336286)
XLA Ops:
  0.6 73.0 %muon_step.1 = (bf16[6,512,256]{2,1,0:T(8,128)(2,1)S(1)}, f32[6,8,256]{2,1,0:T(8,128)S(1)}, f32[6,8,256]{2,1,0:T(8,128)S(1)}, bf16[2,512,256]{2,1,0:T(8,128)(2,1)S(1)}, f32[1,2]{1,0:T(1,128)S(1)}) custom-call(s32[6]{0:T(128)} %refs_0_.1, bf16[6,512,256]{2,1,0:T(8,128)(2,1)} %bitcast.2, f32[6,8,256]{2,1,0:T(8,128)} %refs_2_.1, f32[6,8,256]{2,1,0:T(8,128)} %refs_3_.1), custom_call_target="tpu_custom_call" | custom-call | tf_op jit(solution)/shard_map/muon_step/pallas_call | solution.py:505
  73.7 1.4 %write_out.1 = (bf16[6,512,256]{2,1,0:T(8,128)(2,1)}, f32[6,8,256]{2,1,0:T(8,128)}, f32[6,8,256]{2,1,0:T(8,128)}, bf16[2,512,256]{2,1,0:T(8,128)(2,1)}, f32[1,2]{1,0:T(1,128)}) custom-call(bf16[6,512,256]{2,1,0:T(8,128)(2,1)S(1)} %get-tuple-element.15.refs_0_, f32[6,8,256]{2,1,0:T(8,128)S(1)} %get-tuple-element.16.refs_1_, ...), custom_call_target="tpu_custom_call" | custom-call | tf_op jit(solution)/shard_map/write_out/pallas_call | solution.py:536

commit v4 on v3

--- a/solution.py
+++ b/solution.py
@@ -31,7 +31,7 @@
 NEAR = (0, 1, 7, 2, 6, 3, 5, 4)
 
 BUFFERS = dict(
-    own_g=((NM, KV, 128), bf16),
+    gv=((NM, KV, 256), bf16),
     sib_g=((NM, KV, 128), bf16),
     sum1=((NM, NX, 128, 128), bf16),
     xr=((NM, NX - 1, 128, 128), bf16),
@@ -132,7 +132,7 @@
         pending.clear()
 
     loc = [
-        local(0, g.at[:, :, cols(c)], B["own_g"]),
+        local(0, g, B["gv"]),
         local(1, mom.at[:, :, cols(c)], B["mom16"].at[:, rows8(c), :]),
         local(2, mas.at[:, :, cols(c)], B["mas16"].at[:, rows8(c), :]),
         local(3, mas, B["mas"]),
@@ -147,6 +147,8 @@
         pl.semaphore_signal(barrier, inc=1, device_id=to, device_id_type=pl.DeviceIdType.MESH)
     pl.semaphore_wait(barrier, len(partners))
     ow_out[...] = jnp.zeros_like(ow_out)
+    for item in loc:
+        item.wait()
     yield "barrier", flush
 
     def each(order, op):
@@ -160,12 +162,10 @@
     sma.start()
 
     def swap(m, delta):
-        remote("sg", g.at[m, :, cols(oc)], B["sib_g"].at[m], sib, recv=m).start()
+        remote("sg", B["gv"].at[m, :, cols(oc)], B["sib_g"].at[m], sib, recv=m).start()
 
     each(FAR, swap)
     pending += [lambda: sent("sg", B["sib_g"]), smo.wait_send, sma.wait_send]
-    for item in loc:
-        item.wait()
 
     def pair(m, delta):
         received("sg", B["sib_g"].at[m], recv=m)
@@ -173,7 +173,7 @@
         def add(xx, carry):
             for yy in range(NY):
                 rows = rows16(yy * 4 + xx)
-                total = B["own_g"][m, rows, :].astype(f32) + B["sib_g"][m, rows, :].astype(f32)
+                total = B["gv"][m, rows, cols(c)].astype(f32) + B["sib_g"][m, rows, :].astype(f32)
                 B["sum1"][m, xx, pl.ds(yy * 16, 16), :] = total.astype(bf16)
             return carry
 
@@ -398,7 +398,7 @@
 
     @pl.when(worker)
     def _():
-        for k in (4, 3, 5, 2, 6, 1, 7):
+        for k in NEAR[1:]:
             remote("sy", B["big"].at[c, y, x], B["big"].at[c, y, x], ypeer(k), recv=y).start()
 
     def drain_worker():
@@ -461,15 +461,6 @@
             B["mas"][m, :, cols(cc)] * (1.0 - learn_rate * weight_decay) - learn_rate * own
         )
 
-    def to_sibling(m, delta):
-        received("sx", B["big"].at[c, m, pl.ds(0, NX - 1)], recv=m)
-        remote("sc", B["big"].at[c, m], B["big"].at[c, m], sib, recv=m).start()
-        finish(c, m)
-
-    each(NEAR, to_sibling)
-    pending.append(lambda: sent("sc", B["big"].at[c]))
-    yield "sx", flush
-
     for m in range(NM):
         not_mine(lambda m: received("sq", B["sqr"].at[m], recv=m), m)
     lane = lax.broadcasted_iota(jnp.int32, (1, 128), 1)
@@ -481,11 +472,21 @@
             rms = rms + jnp.where(chosen[s] & (lane == s), value, 0.0)
     rms_out[...] = rms[:, 0:MOST]
 
+    def to_sibling(m, delta):
+        received("sx", B["big"].at[c, m, pl.ds(0, NX - 1)], recv=m)
+        remote("sc", B["big"].at[c, m], B["big"].at[c, m], sib, recv=m).start()
+
     def from_sibling(m, delta):
         received("sc", B["big"].at[oc, m], recv=m)
         finish(oc, m)
 
-    each(NEAR, from_sibling)
+    for i, delta in enumerate(NEAR):
+        each((delta,), to_sibling)
+        if i:
+            each((NEAR[i - 1],), from_sibling)
+        each((delta,), lambda m, delta: finish(c, m))
+    each((NEAR[-1],), from_sibling)
+    pending.append(lambda: sent("sc", B["big"].at[c]))
     flush()
 
 

time: 75.2 us -> 74.3 us (0.988)
  the two profiles are of different devices: /device:TPU:57 before, /device:TPU:1 now
where the time goes in v4:
time: 74.3 us; the launch traced here: 74.1 us
  Pallas kernels  73.5 us (99%)
    pallas_call x1, Pallas kernels, step(): pl.pallas_call(functools.partial(kernel, stop), out_shape=(pltpu.VMEM((NM...  72.1 us

profile of v4, /device:TPU:1, one launch (start us, length us, event | category | flops | bytes accessed | tf_op | source)
XLA Modules:
  0.0 74.1 jit_solution(6454664671690516888)
XLA Ops:
  0.6 72.1 %muon_step.1 = (bf16[6,512,256]{2,1,0:T(8,128)(2,1)S(1)}, f32[6,8,256]{2,1,0:T(8,128)S(1)}, f32[6,8,256]{2,1,0:T(8,128)S(1)}, bf16[2,512,256]{2,1,0:T(8,128)(2,1)S(1)}, f32[1,2]{1,0:T(1,128)S(1)}) custom-call(s32[6]{0:T(128)} %refs_0_.1, bf16[6,512,256]{2,1,0:T(8,128)(2,1)} %bitcast.2, f32[6,8,256]{2,1,0:T(8,128)} %refs_2_.1, f32[6,8,256]{2,1,0:T(8,128)} %refs_3_.1), custom_call_target="tpu_custom_call" | custom-call | tf_op jit(solution)/shard_map/muon_step/pallas_call | solution.py:506
  72.7 1.4 %write_out.1 = (bf16[6,512,256]{2,1,0:T(8,128)(2,1)}, f32[6,8,256]{2,1,0:T(8,128)}, f32[6,8,256]{2,1,0:T(8,128)}, bf16[2,512,256]{2,1,0:T(8,128)(2,1)}, f32[1,2]{1,0:T(1,128)}) custom-call(bf16[6,512,256]{2,1,0:T(8,128)(2,1)S(1)} %get-tuple-element.15.refs_0_, f32[6,8,256]{2,1,0:T(8,128)S(1)} %get-tuple-element.16.refs_1_, ...), custom_call_target="tpu_custom_call" | custom-call | tf_op jit(solution)/shard_map/write_out/pallas_call | solution.py:537

commit v5 on v4

--- a/solution.py
+++ b/solution.py
@@ -63,13 +63,13 @@
     mb=((2, NX, NY, NM, 16, 128), bf16),
 )
 PHASES = dict(
-    loc=(4, 1), sg=(1, NM), smo=(1, 1), sma=(1, 1), x1=(1, NM), y1=(7, 1), my=(7, 1),
-    ay=(1, 1), ux=(1, 1), gs=(1, 1), zr=(1, 1), za=(1, 1), gx=(1, 1), gc=(1, 1), ax=(1, 1),
+    loc=(5, 1), sg=(1, NM), smo=(1, 1), sma=(1, 1), x1=(1, NM), y1=(7, 1), my=(7, 1),
+    ay=(1, 1), ux=(1, 1), gs=(1, 1), zr=(1, 1), za=(1, 1), gx=(1, 1), gc=(1, 1), ax=(2, 2),
     ac=(1, 1), ny=(8, NM), ns=(1, 1), sq=(8, NM), sy=(1, NM), sx=(1, NM), sc=(1, NM),
 )
 
 
-def stages(owners, g, mom, mas, w_out, nm_out, ma_out, ow_out, rms_out, *scratch):
+def stages(ids, g, mom, mas, w_out, nm_out, ma_out, ow_out, rms_out, owners, *scratch):
     names = list(BUFFERS)
     B = dict(zip(names, scratch[: len(names)]))
     sems = scratch[len(names):]
@@ -131,24 +131,23 @@
             wait()
         pending.clear()
 
+    barrier = pltpu.get_barrier_semaphore()
+    partners = [step(k) for k in (4, 3, 5, 2, 6, 1, 7) for step in (zpeer, ypeer)]
+    partners += [xpeer(k) for k in (2, 1, 3)] + [sib]
+    for to in partners:
+        pl.semaphore_signal(barrier, inc=1, device_id=to, device_id_type=pl.DeviceIdType.MESH)
     loc = [
         local(0, g, B["gv"]),
         local(1, mom.at[:, :, cols(c)], B["mom16"].at[:, rows8(c), :]),
         local(2, mas.at[:, :, cols(c)], B["mas16"].at[:, rows8(c), :]),
         local(3, mas, B["mas"]),
+        local(4, ids, owners),
     ]
     for item in loc:
         item.start()
-
-    barrier = pltpu.get_barrier_semaphore()
-    partners = [sib] + [xpeer(k) for k in range(1, NX)]
-    partners += [ypeer(k) for k in range(1, NY)] + [zpeer(k) for k in range(1, NZ)]
-    for to in partners:
-        pl.semaphore_signal(barrier, inc=1, device_id=to, device_id_type=pl.DeviceIdType.MESH)
+    ow_out[...] = jnp.zeros_like(ow_out)
+    loc[0].wait()
     pl.semaphore_wait(barrier, len(partners))
-    ow_out[...] = jnp.zeros_like(ow_out)
-    for item in loc:
-        item.wait()
     yield "barrier", flush
 
     def each(order, op):
@@ -165,6 +164,8 @@
         remote("sg", B["gv"].at[m, :, cols(oc)], B["sib_g"].at[m], sib, recv=m).start()
 
     each(FAR, swap)
+    for item in loc[1:]:
+        item.wait()
     pending += [lambda: sent("sg", B["sib_g"]), smo.wait_send, sma.wait_send]
 
     def pair(m, delta):
@@ -282,10 +283,15 @@
     yield "gs", flush
 
     received("ay", B["mb"].at[c, x, pl.ds(0, NY - 1)])
-    for k in range(1, NX):
-        remote("ax", B["mb"].at[c, x], B["mb"].at[c, x], xpeer(k)).start()
+    def ax(k, part):
+        return remote(
+            "ax", B["mb"].at[c, x], B["mb"].at[c, x], xpeer(k), send=part, recv=part
+        )
+
+    ax(1, 0).start()
+    ax(3, 0).start()
     flush()
-    pending.append(lambda: sent("ax", B["mb"].at[c, pl.ds(0, NX - 1)]))
+    pending.append(lambda: sent("ax", B["mb"].at[c, pl.ds(0, 2)], send=0))
 
     def drain_head():
         sent("ux", B["u"].at[pl.ds(0, NX - 1)])
@@ -307,6 +313,10 @@
         B["gz"][z] = total.astype(bf16)
         for k in (4, 3, 5, 2, 6, 1, 7):
             remote("za", B["gz"].at[z], B["gz"].at[z], zpeer(k)).start()
+
+    ax(2, 1).start()
+    pending.append(ax(2, 1).wait_send)
+
     pending.append(lambda: pl.when(worker)(lambda: sent("za", B["gz"].at[pl.ds(0, NZ - 1)])))
     yield "zr", flush
 
@@ -330,7 +340,8 @@
     pending.append(lambda: pl.when(worker)(lambda: sent("gc", B["g4"].at[c])))
     yield "gx", flush
 
-    received("ax", B["mb"].at[c, pl.ds(0, NX - 1)])
+    received("ax", B["mb"].at[c, pl.ds(0, 2)], recv=0)
+    received("ax", B["mb"].at[c, x], recv=1)
     ac = remote("ac", B["mb"].at[c], B["mb"].at[c], sib)
     ac.start()
     pending.append(ac.wait_send)
@@ -396,10 +407,20 @@
         B["big"][c, y, x] = (factor * last.astype(f32)).astype(bf16)
     yield "ns", flush
 
-    @pl.when(worker)
-    def _():
-        for k in NEAR[1:]:
-            remote("sy", B["big"].at[c, y, x], B["big"].at[c, y, x], ypeer(k), recv=y).start()
+    def sy(k):
+        return remote("sy", B["big"].at[c, y, x], B["big"].at[c, y, x], ypeer(k), recv=y)
+
+    def sx(m):
+        for k in (2, 1, 3):
+            remote("sx", B["big"].at[c, m, x], B["big"].at[c, m, x], xpeer(k), recv=m).start()
+
+    @pl.when(worker)
+    def _():
+        sy(1).start()
+        sy(7).start()
+        sx(y)
+        sy(2).start()
+        sy(6).start()
 
     def drain_worker():
         sent("sy", B["yr"])
@@ -419,23 +440,37 @@
     ns.wait_recv()
     nm_out[:, :, cols(oc)] = B["nmsib"][...]
 
-    def on_x(m, delta):
-        if delta:
-            received("sy", B["big"].at[c, m, x], recv=m)
-        for k in (2, 1, 3):
-            remote("sx", B["big"].at[c, m, x], B["big"].at[c, m, x], xpeer(k), recv=m).start()
-
-    each(NEAR, on_x)
-    pending.append(lambda: pl.when(worker)(drain_worker))
-    pending.append(lambda: sent("sx", B["xr"]))
-    yield "sy", flush
-
     def picks(m):
         mine = owners[m]
         slot = jnp.int32(0)
         for j in range(NM):
             slot = slot + ((owners[j] == mine) & (j < m)).astype(jnp.int32)
         return [(mine == d) & (slot == s) for s in range(MOST)]
+
+    for m in range(NM):
+        not_mine(lambda m: received("sq", B["sqr"].at[m], recv=m), m)
+    lane = lax.broadcasted_iota(jnp.int32, (1, 128), 1)
+    rms = jnp.zeros((1, 128), f32)
+    for m in range(NM):
+        value = jnp.sqrt(B["sqr"][m, 0:1, :] / float(KV * D))
+        chosen = picks(m)
+        for s in range(MOST):
+            rms = rms + jnp.where(chosen[s] & (lane == s), value, 0.0)
+    rms_out[...] = rms[:, 0:MOST]
+
+    @pl.when(worker)
+    def _():
+        for k in (3, 5, 4):
+            sy(k).start()
+
+    def on_x(m, delta):
+        received("sy", B["big"].at[c, m, x], recv=m)
+        sx(m)
+
+    each(NEAR[1:], on_x)
+    pending.append(lambda: pl.when(worker)(drain_worker))
+    pending.append(lambda: sent("sx", B["xr"]))
+    yield "sy", flush
 
     def finish(cc, m):
         chosen = picks(m)
@@ -461,17 +496,6 @@
             B["mas"][m, :, cols(cc)] * (1.0 - learn_rate * weight_decay) - learn_rate * own
         )
 
-    for m in range(NM):
-        not_mine(lambda m: received("sq", B["sqr"].at[m], recv=m), m)
-    lane = lax.broadcasted_iota(jnp.int32, (1, 128), 1)
-    rms = jnp.zeros((1, 128), f32)
-    for m in range(NM):
-        value = jnp.sqrt(B["sqr"][m, 0:1, :] / float(KV * D))
-        chosen = picks(m)
-        for s in range(MOST):
-            rms = rms + jnp.where(chosen[s] & (lane == s), value, 0.0)
-    rms_out[...] = rms[:, 0:MOST]
-
     def to_sibling(m, delta):
         received("sx", B["big"].at[c, m, pl.ds(0, NX - 1)], recv=m)
         remote("sc", B["big"].at[c, m], B["big"].at[c, m], sib, recv=m).start()
@@ -500,7 +524,8 @@
 def step(owners, g, mom, mas, stop=None, collective_id=0):
     vmem = pl.BlockSpec(memory_space=pltpu.VMEM)
     hbm = pl.BlockSpec(memory_space=pltpu.HBM)
-    scratch = [pltpu.VMEM(*spec) for spec in BUFFERS.values()]
+    scratch = [pltpu.SMEM((NM,), jnp.int32)]
+    scratch += [pltpu.VMEM(*spec) for spec in BUFFERS.values()]
     for send, recv in PHASES.values():
         scratch += [pltpu.SemaphoreType.DMA((send,)), pltpu.SemaphoreType.DMA((recv,))]
     return pl.pallas_call(
@@ -512,7 +537,7 @@
             pltpu.VMEM((MOST, KV, 256), bf16),
             pltpu.VMEM((1, MOST), f32),
         ),
-        in_specs=[pl.BlockSpec(memory_space=pltpu.SMEM), hbm, hbm, hbm],
+        in_specs=[hbm, hbm, hbm, hbm],
         out_specs=(vmem, vmem, vmem, vmem, vmem),
         scratch_shapes=scratch,
         compiler_params=pltpu.CompilerParams(

time: 74.3 us -> 73.8 us (level)
  no operation moved by 1% of the time
where the time goes in v5:
time: 73.8 us; the launch traced here: 73.7 us
  Pallas kernels  73 us (99%)
    pallas_call x1, Pallas kernels, step(): pl.pallas_call(functools.partial(kernel, stop), out_shape=(pltpu.VMEM((NM...  71.6 us

profile of v5, /device:TPU:1, one launch (start us, length us, event | category | flops | bytes accessed | tf_op | source)
XLA Modules:
  0.0 73.7 jit_solution(12547975308878226387)
XLA Ops:
  0.6 71.6 %muon_step.1 = (bf16[6,512,256]{2,1,0:T(8,128)(2,1)S(1)}, f32[6,8,256]{2,1,0:T(8,128)S(1)}, f32[6,8,256]{2,1,0:T(8,128)S(1)}, bf16[2,512,256]{2,1,0:T(8,128)(2,1)S(1)}, f32[1,2]{1,0:T(1,128)S(1)}) custom-call(s32[6]{0:T(128)} %refs_0_.1, bf16[6,512,256]{2,1,0:T(8,128)(2,1)} %bitcast.2, f32[6,8,256]{2,1,0:T(8,128)} %refs_2_.1, f32[6,8,256]{2,1,0:T(8,128)} %refs_3_.1), custom_call_target="tpu_custom_call" | custom-call | tf_op jit(solution)/shard_map/muon_step/pallas_call | solution.py:531
  72.3 1.4 %write_out.1 = (bf16[6,512,256]{2,1,0:T(8,128)(2,1)}, f32[6,8,256]{2,1,0:T(8,128)}, f32[6,8,256]{2,1,0:T(8,128)}, bf16[2,512,256]{2,1,0:T(8,128)(2,1)}, f32[1,2]{1,0:T(1,128)}) custom-call(bf16[6,512,256]{2,1,0:T(8,128)(2,1)S(1)} %get-tuple-element.15.refs_0_, f32[6,8,256]{2,1,0:T(8,128)S(1)} %get-tuple-element.16.refs_1_, ...), custom_call_target="tpu_custom_call" | custom-call | tf_op jit(solution)/shard_map/write_out/pallas_call | solution.py:562

commit v6 on v5

--- a/solution.py
+++ b/solution.py
@@ -64,7 +64,7 @@
 )
 PHASES = dict(
     loc=(5, 1), sg=(1, NM), smo=(1, 1), sma=(1, 1), x1=(1, NM), y1=(7, 1), my=(7, 1),
-    ay=(1, 1), ux=(1, 1), gs=(1, 1), zr=(1, 1), za=(1, 1), gx=(1, 1), gc=(1, 1), ax=(2, 2),
+    ay=(1, 1), ux=(1, 1), gs=(1, 1), zr=(1, 1), za=(1, 1), gx=(1, NX - 1), gc=(1, 1), ax=(2, 2),
     ac=(1, 1), ny=(8, NM), ns=(1, 1), sq=(8, NM), sy=(1, NM), sx=(1, NM), sc=(1, NM),
 )
 
@@ -320,6 +320,10 @@
     pending.append(lambda: pl.when(worker)(lambda: sent("za", B["gz"].at[pl.ds(0, NZ - 1)])))
     yield "zr", flush
 
+    def gc(k):
+        part = B["g4"].at[c, (x + NX - k) % NX]
+        return remote("gc", part, part, sib)
+
     @pl.when(worker)
     def _():
         received("za", B["gz"].at[pl.ds(0, NZ - 1)])
@@ -327,16 +331,17 @@
             at, to = (p // 2) * 16, (p % 2) * 256
             B["g4"][c, x, at:at + 16, to:to + 256] = B["gz"][p]
         for k in (2, 1, 3):
-            remote("gx", B["g4"].at[c, x], B["g4"].at[c, x], xpeer(k)).start()
+            remote("gx", B["g4"].at[c, x], B["g4"].at[c, x], xpeer(k), recv=k - 1).start()
+        gc(0).start()
     pending.append(lambda: pl.when(worker)(lambda: sent("gx", B["g4"].at[c, pl.ds(0, NX - 1)])))
     yield "za", flush
 
     @pl.when(worker)
     def _():
-        received("gx", B["g4"].at[c, pl.ds(0, NX - 1)])
-        gc = remote("gc", B["g4"].at[c], B["g4"].at[c], sib)
-        gc.start()
-        gc.wait_recv()
+        for k in (1, 3, 2):
+            received("gx", B["g4"].at[c, (x + NX - k) % NX], recv=k - 1)
+            gc(k).start()
+        received("gc", B["g4"].at[oc])
     pending.append(lambda: pl.when(worker)(lambda: sent("gc", B["g4"].at[c])))
     yield "gx", flush
 

time: 73.8 us -> 73.7 us (level)
  no operation moved by 1% of the time
where the time goes in v6:
time: 73.7 us; the launch traced here: 73.5 us
  Pallas kernels  72.9 us (99%)
    pallas_call x1, Pallas kernels, step(): pl.pallas_call(functools.partial(kernel, stop), out_shape=(pltpu.VMEM((NM...  71.5 us

profile of v6, /device:TPU:1, one launch (start us, length us, event | category | flops | bytes accessed | tf_op | source)
XLA Modules:
  0.0 73.5 jit_solution(155343358537753302)
XLA Ops:
  0.6 71.5 %muon_step.1 = (bf16[6,512,256]{2,1,0:T(8,128)(2,1)S(1)}, f32[6,8,256]{2,1,0:T(8,128)S(1)}, f32[6,8,256]{2,1,0:T(8,128)S(1)}, bf16[2,512,256]{2,1,0:T(8,128)(2,1)S(1)}, f32[1,2]{1,0:T(1,128)S(1)}) custom-call(s32[6]{0:T(128)} %refs_0_.1, bf16[6,512,256]{2,1,0:T(8,128)(2,1)} %bitcast.2, f32[6,8,256]{2,1,0:T(8,128)} %refs_2_.1, f32[6,8,256]{2,1,0:T(8,128)} %refs_3_.1), custom_call_target="tpu_custom_call" | custom-call | tf_op jit(solution)/shard_map/muon_step/pallas_call | solution.py:536
  72.1 1.4 %write_out.1 = (bf16[6,512,256]{2,1,0:T(8,128)(2,1)}, f32[6,8,256]{2,1,0:T(8,128)}, f32[6,8,256]{2,1,0:T(8,128)}, bf16[2,512,256]{2,1,0:T(8,128)(2,1)}, f32[1,2]{1,0:T(1,128)}) custom-call(bf16[6,512,256]{2,1,0:T(8,128)(2,1)S(1)} %get-tuple-element.15.refs_0_, f32[6,8,256]{2,1,0:T(8,128)S(1)} %get-tuple-element.16.refs_1_, ...), custom_call_target="tpu_custom_call" | custom-call | tf_op jit(solution)/shard_map/write_out/pallas_call | solution.py:567
